TPU v7x, 1024 devices: a whole 4x4x32 slice. The times are simulated.
1024 devices in a mesh: dp: 2 (over x_lo), hid: 64 (over z, core), inp: 8 (over y, x_hi).
Axes of the slice: x: 4 (x_hi: 2, x_lo: 2; x = x_hi * 2 + x_lo), y: 4, z: 32, core: 2. Of those that a mesh axis runs over, the one named last changes fastest.
Arguments:
- out_grad: bfloat16 [512, 16384], P(('dp', 'hid'), 'inp'), may hold values from -6 to 6
- gate_act: bfloat16 [512, 32768], P('dp', 'hid'), may hold values from -6 to 6
- up_act: bfloat16 [512, 32768], P('dp', 'hid'), may hold values from -6 to 6
- frames: bfloat16 [512, 1280], P('dp', 'hid'), may hold values from -0.59765625 to 0.59765625
- w_gate: bfloat16 [16384, 32768], P('inp', 'hid'), may hold values from -0.046875 to 0.046875
- w_up: bfloat16 [16384, 32768], P('inp', 'hid'), may hold values from -0.046875 to 0.046875
- w_down: bfloat16 [32768, 16384], P('hid', 'inp'), may hold values from -0.03125 to 0.03125
Outputs:
- input_grad: bfloat16 [512, 16384], P(('dp', 'hid'), 'inp')
- adapter_grad: float32 [1280, 16384], P('hid', 'inp')
All inputs are finite; a program needn't handle non-finite values.
Results may differ from a plain program's by a relative error of at most 0.0049.
Values may be sent and summed in bfloat16 or wider, within the bound.
A program may use at most 32 MiB of HBM per device.

v0:
```python
import jax
import jax.numpy as jnp
from jax import lax
from jax.sharding import PartitionSpec as P


def contract_last(left, right):
    return lax.dot_general(
        left, right, (((1,), (1,)), ((), ())), preferred_element_type=jnp.float32
    )


def contract_first(left, right):
    return lax.dot_general(
        left, right, (((0,), (0,)), ((), ())), preferred_element_type=jnp.float32
    )


def local_grads(hidden_grad, gate_rows, up_rows):
    gate = gate_rows.astype(jnp.float32)
    upper = up_rows.astype(jnp.float32)
    sigma = jax.nn.sigmoid(gate)
    gate_grad = (hidden_grad * upper * sigma * (1.0 + gate * (1.0 - sigma))).astype(jnp.bfloat16)
    up_grad = (hidden_grad * gate * sigma).astype(jnp.bfloat16)
    return (gate_grad, up_grad)


def per_device(out_grad, gate_act, up_act, frames, w_gate, w_up, w_down):
    partial_value = contract_last(lax.all_gather(out_grad, "hid", axis=0, tiled=True), w_down)
    hidden_grad = lax.psum(partial_value, "inp")
    gate_grad, up_grad = local_grads(hidden_grad, gate_act, up_act)
    mine = lax.psum_scatter(
        contract_last(gate_grad, w_gate) + contract_last(up_grad, w_up),
        "hid",
        scatter_dimension=0,
        tiled=True,
    )
    input_grad = mine.astype(jnp.bfloat16)
    adapter_part = contract_first(frames, lax.all_gather(input_grad, "hid", axis=0, tiled=True))
    adapter_grad = lax.psum(adapter_part, "dp")
    return (input_grad, adapter_grad)


def solution(mesh):
    return jax.shard_map(
        per_device,
        mesh=mesh,
        in_specs=(
            P(("dp", "hid"), "inp"),
            P("dp", "hid"),
            P("dp", "hid"),
            P("dp", "hid"),
            P("inp", "hid"),
            P("inp", "hid"),
            P("hid", "inp"),
        ),
        out_specs=(P(("dp", "hid"), "inp"), P("hid", "inp")),
        check_vma=False,
    )
```

profile of v0, /device:TPU:1, one launch (start us, length us, event | category | flops | bytes accessed | tf_op | source)
XLA Modules:
  0.0 678.8 jit_solution(11777896646195891438)
XLA Ops:
  7.2 0.0 copy-start
  7.2 0.0 all-gather.5.cloned.1.call-start
  7.2 0.7 all-gather.5.cloned.1.call-update
  7.9 0.0 all-reduce.5.cloned.1.call-start
  8.0 146.9 %all-gather.5.cloned.1.call-done = bf16[64,4,2048]{2,1,0:T(4,128)(2,1)} async-done(((bf16[1,4,2048]{2,1,0:T(4,128)(2,1)}), bf16[64,4,2048]{2,1,0:T(4,128)(2,1)}) %all-gather.5.cloned.1.call-update) | async-done | bytes 1048592 | tf_op jit(solution)/shard_map/all_gather | solution.py:29
  154.8 1.3 reshape.5
  156.2 0.0 copy-start.4
  156.2 3.2 fusion.15
  159.4 0.0 all-reduce.5.cloned.1.call-update
  159.4 0.0 all-gather.7.cloned.1.call-start
  159.4 1.3 dynamic-slice
  161.4 106.0 %all-reduce.5.cloned.1.call-done = f32[256,512]{1,0:T(8,128)} async-done(((f32[256,512]{1,0:T(8,128)}), f32[256,512]{1,0:T(8,128)}) %all-reduce.5.cloned.1.call-update) | async-done | bytes 524304 | tf_op jit(solution)/shard_map/psum | solution.py:30
  267.3 0.0 copy-done
  267.3 0.0 copy-done.4
  267.3 0.0 copy-start.1
  267.3 0.0 copy-start.3
  267.3 2.1 fusion.9
  269.4 0.0 copy-done.1
  269.4 0.0 copy-done.3
  269.5 2.1 convolution_add_fusion
  271.6 0.0 copy-start.5
  271.6 204.6 %all-reduce.8 = bf16[256,2048]{1,0:T(8,128)(2,1)S(1)} all-reduce(f32[256,2048]{1,0:T(8,128)} %convolution_add_fusion), channel_id=2, replica_groups=mesh['dp'=2,'hid'=64,'inp'=8] {'hid'}, use_global_device_ids=true, to_apply=%region_1.0.clone | all-reduce | flops 524288 | bytes 3145728
  476.1 0.0 copy-start.2
  476.1 0.7 fusion.22
  476.8 0.0 all-gather.7.cloned.1.call-update
  476.8 0.0 all-reduce.7.cloned.1.call-start
  476.9 0.2 copy-done.2
  477.1 133.9 %all-gather.7.cloned.1.call-done = bf16[64,4,2048]{2,1,0:T(4,128)(2,1)} async-done(((bf16[1,4,2048]{2,1,0:T(4,128)(2,1)}), bf16[64,4,2048]{2,1,0:T(4,128)(2,1)}) %all-gather.7.cloned.1.call-update) | async-done | bytes 1048592 | tf_op jit(solution)/shard_map/all_gather | solution.py:39
  611.0 1.3 reshape.7
  612.4 0.0 copy-done.5
  612.4 0.9 convolution_bitcast_fusion
  613.3 0.0 all-reduce.7.cloned.1.call-update
  613.4 1.4 dynamic-slice_convert_fusion
  614.7 55.9 %all-reduce.7.cloned.1.call-done = f32[20,2048]{1,0:T(8,128)} async-done(((f32[20,2048]{1,0:T(8,128)}), f32[20,2048]{1,0:T(8,128)}) %all-reduce.7.cloned.1.call-update) | async-done | bytes 163856 | tf_op jit(solution)/shard_map/psum | solution.py:40
  670.7 1.6 copy.13
Async XLA Ops:
  7.2 260.2 %copy-start = (bf16[2048,512]{1,0:T(8,128)(2,1)S(1)}, bf16[2048,512]{1,0:T(8,128)(2,1)}, u32[]{:S(2)}) copy-start(bf16[2048,512]{1,0:T(8,128)(2,1)} %param.11) | copy-start | bytes 6291460
  7.2 147.7 %all-gather.5.cloned.1.call-start = ((), (), s32[]{:S(2)}) async-start(), calls=%async_computation.2 | async-start | bytes 1064960 | tf_op jit(solution)/shard_map/all_gather | solution.py:29
  7.9 259.4 %all-reduce.5.cloned.1.call-start = ((), (), s32[]{:S(2)}) async-start(), calls=%async_computation | async-start | bytes 1048576 | tf_op jit(solution)/shard_map/psum | solution.py:30
  156.2 111.2 %copy-start.4 = (bf16[256,512]{1,0:T(8,128)(2,1)S(1)}, bf16[256,512]{1,0:T(8,128)(2,1)}, u32[]{:S(2)}) copy-start(bf16[256,512]{1,0:T(8,128)(2,1)} %param.8) | copy-start | bytes 786436
  159.4 451.7 %all-gather.7.cloned.1.call-start = ((), (), s32[]{:S(2)}) async-start(), calls=%async_computation.3 | async-start | bytes 1064960 | tf_op jit(solution)/shard_map/all_gather | solution.py:39
  267.3 2.1 copy-start.1
  267.3 2.1 copy-start.3
  271.6 340.8 %copy-start.5 = (bf16[256,20]{0,1:T(8,128)(2,1)S(1)}, bf16[256,20]{0,1:T(8,128)(2,1)}, u32[]{:S(2)}) copy-start(bf16[256,20]{0,1:T(8,128)(2,1)} %param.10) | copy-start | bytes 30724
  476.1 1.0 copy-start.2
  476.8 193.8 %all-reduce.7.cloned.1.call-start = ((), (), s32[]{:S(2)}) async-start(), calls=%async_computation.1 | async-start | bytes 393216 | tf_op jit(solution)/shard_map/psum | solution.py:40
Sparse Core Ops, SparseCore 0:
  10.7 144.0 all-gather.4
  159.5 107.7 all-reduce.4
  477.0 134.0 all-gather.6
  615.3 55.2 all-reduce.6
where the time goes:
time: 680 us; the launch traced here: 679 us
  waiting for transfers between devices  443 us (65%)
  blocking collectives  205 us (30%)
  between operations  14.5 us (2%)
  matrix products  8.28 us (1%)
  local copies, waits for them, and re-layouts  7.85 us (1%)
    unnamed x1, blocking collectives  205 us
    all_gather x1, waiting for transfers between devices, per_device(): lax.all_gather(out_grad, 'hid', axis=0, tiled=True)  147 us
    all_gather x1, waiting for transfers between devices, per_device(): lax.all_gather(input_grad, 'hid', axis=0, tiled=True)  134 us
    psum x1, waiting for transfers between devices, per_device(): hidden_grad = lax.psum(partial_value, 'inp')  106 us
    psum x1, waiting for transfers between devices, per_device(): adapter_grad = lax.psum(adapter_part, 'dp')  55.9 us
  transfers between devices with their start and end apart: 4, of which 4 were waited for; matrix products, arithmetic and copies ran while one was open for 0% of the time, Pallas kernels for 0%

commit v1 on v0

v1 whole, which is shorter than its diff:
```python
import functools

import jax
import jax.numpy as jnp
from jax import lax
from jax.experimental import pallas as pl
from jax.experimental.pallas import tpu as pltpu
from jax.sharding import PartitionSpec as P

MESH = pl.DeviceIdType.MESH
BF = jnp.bfloat16
F32 = jnp.float32
NEAR = 4


def dot_nt(a, b):
    return lax.dot_general(a, b, (((1,), (1,)), ((), ())), preferred_element_type=F32)


def dot_nn(a, b):
    return lax.dot_general(a, b, (((1,), (0,)), ((), ())), preferred_element_type=F32)


def body(Z, N, *refs):
    (og, gact, uact, frames, wg, wu, wd, ig_out, ad_out,
     abuf, dbuf, full, hpart, hrecv, gu, gact_v, uact_v, wg_v, wu_v, wd_v,
     sibf, sibr, pown, csend, cnear, fsend, cfar, eloc, erem,
     lsem, a_sem, d_sem, hs, hr, gs, gr, ss, sr, ns, nr, fs, fr, es, er) = refs
    K = Z // NEAR
    hid = lax.axis_index("hid")
    z = hid // 2
    c = hid % 2
    inp = lax.axis_index("inp")
    dp = lax.axis_index("dp")
    r = z % NEAR
    k = z // NEAR
    sib = {"hid": 2 * z + 1 - c}
    peer = {"dp": 1 - dp}

    def chip(d):
        return {"hid": 2 * ((z + d + 2 * Z) % Z) + c}

    def chip_at(w):
        return {"hid": 2 * w + c}

    def ring(j):
        return {"inp": (inp + j) % N}

    barrier = pltpu.get_barrier_semaphore()
    offsets = sorted({NEAR * m for m in range(1, K)} | {1, 2, Z - 1, Z - 2})
    for d in offsets:
        pl.semaphore_signal(barrier, inc=1, device_id=chip(d), device_id_type=MESH)
    for j in range(1, N):
        pl.semaphore_signal(barrier, inc=1, device_id=ring(j), device_id_type=MESH)
    pl.semaphore_signal(barrier, inc=1, device_id=sib, device_id_type=MESH)
    pl.semaphore_signal(barrier, inc=1, device_id=peer, device_id_type=MESH)

    mine32 = pl.ds(pl.multiple_of(inp * 32, 32), 32)
    local = [
        pltpu.make_async_copy(og, abuf.at[r, c, k], lsem.at[0]),
        pltpu.make_async_copy(wd, wd_v, lsem.at[1]),
        pltpu.make_async_copy(gact.at[mine32], gact_v, lsem.at[2]),
        pltpu.make_async_copy(uact.at[mine32], uact_v, lsem.at[3]),
        pltpu.make_async_copy(wg, wg_v, lsem.at[4]),
        pltpu.make_async_copy(wu, wu_v, lsem.at[5]),
    ]
    for q in local:
        q.start()

    o = lax.broadcasted_iota(jnp.int32, (256, 256), 0)
    i = lax.broadcasted_iota(jnp.int32, (256, 256), 1)
    to = ((i // 4) % 4) * 64 + ((i // 16) % 2) * 32 + (i // 64) * 8 + ((i // 32) % 2) * 4 + i % 4
    perm = jnp.where(o == to, 1.0, 0.0).astype(BF)
    rows = Z * 8
    row = lax.broadcasted_iota(jnp.int32, (rows, 2 * rows), 0)
    col = lax.broadcasted_iota(jnp.int32, (rows, 2 * rows), 1)
    src = 8 * (NEAR * ((col // 16) % K) + col // (16 * K)) + col % 8
    half = (col // 8) % 2
    fr_t = frames[...]
    f0 = dot_nn(fr_t, jnp.where((row == src) & (half == 0), 1.0, 0.0).astype(BF)).astype(BF)
    f1 = dot_nn(fr_t, jnp.where((row == src) & (half == 1), 1.0, 0.0).astype(BF)).astype(BF)

    local[0].wait()
    pl.semaphore_wait(barrier, len(offsets) + N + 1)

    sent = []

    def remote(s, d, send, recv, dev):
        return pltpu.make_async_remote_copy(
            src_ref=s, dst_ref=d, send_sem=send, recv_sem=recv, device_id=dev, device_id_type=MESH
        )

    def launch(*args):
        q = remote(*args)
        q.start()
        sent.append(q)

    def gather(buf, sem):
        mine = buf.at[r, c, k]
        for m in sorted(range(1, K), key=lambda m: -min(m, K - m)):
            launch(mine, mine, sem.at[0, m], sem.at[1, m], chip(NEAR * m))
        for m in sorted(range(1, K), key=lambda m: min(m, K - m)):
            got = buf.at[r, c, (k - m + K) % K]
            remote(got, got, sem.at[0, m], sem.at[1, m], chip(NEAR * m)).wait_recv()
        group = buf.at[r, c]
        two = 2 - 4 * c
        for n, d in enumerate((two, 1, -1)):
            launch(group, group, sem.at[2, n], sem.at[3, n], chip(d))
        launch(group, group, sem.at[4, 3], sem.at[5, 3], sib)
        for n, d in ((1, 1), (2, -1), (0, two)):
            got = buf.at[(r - d + NEAR) % NEAR, c]
            remote(got, got, sem.at[2, n], sem.at[3, n], chip(d)).wait_recv()
            launch(got, got, sem.at[4, n], sem.at[5, n], sib)
        for n, d in ((3, 0), (1, 1), (2, -1), (0, 2)):
            got = buf.at[(r - d + NEAR) % NEAR, 1 - c]
            remote(got, got, sem.at[4, n], sem.at[5, n], sib).wait_recv()

    gather(abuf, a_sem)

    for j in range(K // 2):
        rows_in = abuf[:, :, 2 * j : 2 * j + 2].reshape(256, 512)
        out = dot_nn(perm, rows_in).astype(BF)
        for q in range(4):
            full[64 * j : 64 * j + 64, 512 * q : 512 * q + 512] = out[64 * q : 64 * q + 64]
    local[1].wait()
    hpart[...] = dot_nt(full[...], wd_v[...]).reshape(hpart.shape)

    for j in range(1, N):
        launch(hpart.at[(inp + j) % N], hrecv.at[j - 1], hs.at[j], hr.at[j], ring(j))
    local[2].wait()
    local[3].wait()
    gate = gact_v[...].astype(F32)
    upper = uact_v[...].astype(F32)
    sigma = jax.nn.sigmoid(gate)
    total = hpart[inp]
    for j in range(1, N):
        remote(hpart.at[(inp + j) % N], hrecv.at[j - 1], hs.at[j], hr.at[j], ring(j)).wait_recv()
        total = total + hrecv[j - 1]
    gu[inp, 0] = (total * upper * sigma * (1.0 + gate * (1.0 - sigma))).astype(BF)
    gu[inp, 1] = (total * gate * sigma).astype(BF)
    for j in range(1, N):
        launch(gu.at[inp], gu.at[inp], gs.at[j], gr.at[j], ring(j))
    local[4].wait()
    local[5].wait()
    for j in range(1, N):
        got = gu.at[(inp - j + N) % N]
        remote(got, got, gs.at[j], gr.at[j], ring(j)).wait_recv()

    gg = gu[:, 0].reshape(256, 512)
    ug = gu[:, 1].reshape(256, 512)

    def part(start):
        w = pl.ds(pl.multiple_of(start, 512), 512)
        return (dot_nt(gg, wg_v[w, :]) + dot_nt(ug, wu_v[w, :])).reshape(K, NEAR, 8, 512)

    for h in range(2):
        sibf[h] = part((1 - c) * 1024 + h * 512)
        launch(sibf.at[h], sibr.at[h], ss.at[h], sr.at[h], sib)
    for h in range(2):
        pown[h] = part(c * 1024 + h * 512)
    for h in range(2):
        remote(sibf.at[h], sibr.at[h], ss.at[h], sr.at[h], sib).wait_recv()
        for s in range(NEAR):
            both = pown[h, :, s] + sibr[h, :, s]
            pown[h, :, s] = both
    for s in range(NEAR):
        csend[s] = jnp.concatenate([pown[0, :, s], pown[1, :, s]], axis=1).astype(BF)

    two = 2 - 4 * c
    for n, d in enumerate((two, 1, -1)):
        launch(csend.at[(r + d + NEAR) % NEAR], cnear.at[n], ns.at[n], nr.at[n], chip(d))
    acc = jnp.concatenate([pown[0, :, r], pown[1, :, r]], axis=1)
    for n, d in ((1, 1), (2, -1), (0, two)):
        remote(csend.at[0], cnear.at[n], ns.at[n], nr.at[n], chip(d)).wait_recv()
        acc = acc + cnear[n].astype(F32)
    fsend[...] = acc.astype(BF)
    for m in sorted(range(1, K), key=lambda m: -min(m, K - m)):
        launch(fsend.at[(k + m) % K], cfar.at[m - 1], fs.at[m], fr.at[m], chip(NEAR * m))
    total = jnp.concatenate([pown[0, k, r], pown[1, k, r]], axis=0)
    for n in range(3):
        total = total + cnear[n, k].astype(F32)
    for m in sorted(range(1, K), key=lambda m: min(m, K - m)):
        remote(fsend.at[0], cfar.at[m - 1], fs.at[m], fr.at[m], chip(NEAR * m)).wait_recv()
        total = total + cfar[m - 1].astype(F32)
    dbuf[r, c, k] = total.astype(BF)

    gather(dbuf, d_sem)

    for a in range(2):
        blk = dbuf[r, a, k].astype(F32)
        ig_out[:, 1024 * a : 1024 * a + 512] = blk[0:8]
        ig_out[:, 1024 * a + 512 : 1024 * a + 1024] = blk[8:16]
        x = dbuf[:, a].reshape(2 * rows, 512)
        eloc[0:20, 1024 * a : 1024 * a + 512] = dot_nn(f0, x)
        eloc[0:20, 1024 * a + 512 : 1024 * a + 1024] = dot_nn(f1, x)
    eloc[20:24, :] = jnp.zeros((4, 2048), F32)
    launch(eloc, erem, es, er, peer)
    remote(eloc, erem, es, er, peer).wait_recv()
    ad_out[...] = eloc[0:20, :] + erem[0:20, :]
    for q in sent:
        q.wait_send()


def per_device(Z, N, out_grad, gate_act, up_act, frames, w_gate, w_up, w_down):
    K = Z // NEAR
    og = out_grad.reshape(4, 4, 512).transpose(1, 0, 2).reshape(16, 512)
    hbm = pl.BlockSpec(memory_space=pl.ANY)
    vmem = pl.BlockSpec(memory_space=pltpu.VMEM)
    dma = pltpu.SemaphoreType.DMA
    ig8, ad = pl.pallas_call(
        functools.partial(body, Z, N),
        out_shape=(jax.ShapeDtypeStruct((8, 2048), F32), jax.ShapeDtypeStruct((20, 2048), F32)),
        in_specs=[hbm, hbm, hbm, vmem, hbm, hbm, hbm],
        out_specs=(vmem, vmem),
        scratch_shapes=[
            pltpu.VMEM((NEAR, 2, K, 16, 512), BF),
            pltpu.VMEM((NEAR, 2, K, 16, 512), BF),
            pltpu.VMEM((256, 2048), BF),
            pltpu.VMEM((N, 32, 512), F32),
            pltpu.VMEM((N - 1, 32, 512), F32),
            pltpu.VMEM((N, 2, 32, 512), BF),
            pltpu.VMEM((32, 512), BF),
            pltpu.VMEM((32, 512), BF),
            pltpu.VMEM((2048, 512), BF),
            pltpu.VMEM((2048, 512), BF),
            pltpu.VMEM((512, 2048), BF),
            pltpu.VMEM((2, K, NEAR, 8, 512), F32),
            pltpu.VMEM((2, K, NEAR, 8, 512), F32),
            pltpu.VMEM((2, K, NEAR, 8, 512), F32),
            pltpu.VMEM((NEAR, K, 16, 512), BF),
            pltpu.VMEM((3, K, 16, 512), BF),
            pltpu.VMEM((K, 16, 512), BF),
            pltpu.VMEM((K - 1, 16, 512), BF),
            pltpu.VMEM((24, 2048), F32),
            pltpu.VMEM((24, 2048), F32),
            dma((6,)),
            dma((6, 8)),
            dma((6, 8)),
            dma((8,)),
            dma((8,)),
            dma((8,)),
            dma((8,)),
            dma((2,)),
            dma((2,)),
            dma((3,)),
            dma((3,)),
            dma((8,)),
            dma((8,)),
            dma,
            dma,
        ],
        compiler_params=pltpu.CompilerParams(
            collective_id=0, has_side_effects=True, vmem_limit_bytes=48 * 1024 * 1024
        ),
        cost_estimate=pl.CostEstimate(flops=1_700_000_000, bytes_accessed=8_000_000, transcendentals=0),
    )(og, gate_act, up_act, frames.T, w_gate, w_up, w_down)
    core = lax.axis_index("hid") % 2
    input_grad = lax.dynamic_slice_in_dim(ig8, core * 4, 4, 0).astype(BF)
    return input_grad, ad


def solution(mesh):
    Z = mesh.shape["hid"] // 2
    N = mesh.shape["inp"]
    return jax.shard_map(
        functools.partial(per_device, Z, N),
        mesh=mesh,
        in_specs=(
            P(("dp", "hid"), "inp"),
            P("dp", "hid"),
            P("dp", "hid"),
            P("dp", "hid"),
            P("inp", "hid"),
            P("inp", "hid"),
            P("hid", "inp"),
        ),
        out_specs=(P(("dp", "hid"), "inp"), P("hid", "inp")),
        check_vma=False,
    )
```

time: 680 us -> 140 us (0.21)
  waiting for transfers between devices: 443 us -> 0 us
  blocking collectives: 205 us -> 0 us
  Pallas kernels: 0 us -> 131 us
  between operations: 14.5 us -> 0.66 us
  matrix products: 8.28 us -> 0 us
    all_gather x2 -> x0, waiting for transfers between devices: 281 us -> none  [the longest x1 147 us: per_device(): lax.all_gather(out_grad, 'hid', axis=0, tiled=True)]
    unnamed x1 -> x0, blocking collectives: 205 us -> none
    psum x2 -> x0, waiting for transfers between devices: 162 us -> none  [the longest x1 106 us: per_device(): hidden_grad = lax.psum(partial_value, 'inp')]
    pallas_call x0 -> x1, Pallas kernels: none -> 131 us  [per_device(): pl.pallas_call(functools.partial(body, Z, N), out_shape=(jax.ShapeDtypeSt...]
    dot_general x4 -> x0, matrix products: 8.28 us -> none  [the longest x3 7.35 us: contract_last(): lax.dot_general(left, right, (((1,), (1,)), ((), ())), preferred_element_...]
  transfers between devices with their start and end apart: 4 -> 0, of which waited for: 4 -> 0; matrix products, arithmetic and copies ran while one was open for 0% -> 0% of each run, Pallas kernels for 0% -> 0%
where the time goes in v1:
time: 140 us
  Pallas kernels  131 us (94%)
  local copies, waits for them, and re-layouts  7.81 us (6%)
    pallas_call x1, Pallas kernels, per_device(): pl.pallas_call(functools.partial(body, Z, N), out_shape=(jax.ShapeDtypeSt...  131 us
    unnamed x11, local copies, waits for them, and re-layouts  6.46 us

profile of v1, /device:TPU:1, one launch (start us, length us, event | category | flops | bytes accessed | tf_op | source)
XLA Modules:
  0.0 139.7 jit_solution(1495802955531561190)
XLA Ops:
  0.6 0.7 reshape.11.refs_0_
  1.4 0.0 copy-start
  1.4 1.6 %copy-done = bf16[2048,512]{1,0:T(8,128)(2,1)S(1)} copy-done((bf16[2048,512]{1,0:T(8,128)(2,1)S(1)}, bf16[2048,512]{1,0:T(8,128)(2,1)}, u32[]{:S(2)}) %copy-start) | copy-done | bytes 2097176
  3.0 0.0 copy-start.1
  3.0 1.6 %copy-done.1 = bf16[2048,512]{1,0:T(8,128)(2,1)S(1)} copy-done((bf16[2048,512]{1,0:T(8,128)(2,1)S(1)}, bf16[2048,512]{1,0:T(8,128)(2,1)}, u32[]{:S(2)}) %copy-start.1) | copy-done | bytes 2097176
  4.6 0.0 copy-start.2
  4.6 0.9 copy-done.2
  5.5 0.0 copy-start.3
  5.5 0.9 copy-done.3
  6.5 0.0 copy-start.4
  6.5 0.7 copy-done.4
  7.2 131.2 %shard_map.86 = (f32[8,2048]{1,0:T(8,128)S(1)}, f32[20,2048]{1,0:T(8,128)S(1)}) custom-call(bf16[16,512]{1,0:T(8,128)(2,1)S(1)} %reshape.11.refs_0_, bf16[256,512]{1,0:T(8,128)(2,1)S(1)} %copy-done.2, bf16[256,512]{1,0:T(8,128)(2,1)S(1)} %copy-done.3, bf16[20,256]{1,0:T(8,128)(2,1)S(1)} %bitcast.4, bf16[2048,512]{1,0:T(8,128)(2,1)S(1)} %copy-done, ...), custom_call_target="tpu_custom_call" | custom-call | flops 1700000000 | bytes 8000000 | tf_op jit(solution)/shard_map/pallas_call | solution.py:210
  138.4 0.6 dynamic-slice_convert_fusion
  139.0 0.7 copy.11
Async XLA Ops:
  1.4 1.6 %copy-start = (bf16[2048,512]{1,0:T(8,128)(2,1)S(1)}, bf16[2048,512]{1,0:T(8,128)(2,1)}, u32[]{:S(2)}) copy-start(bf16[2048,512]{1,0:T(8,128)(2,1)} %refs_4_.1) | copy-start | bytes 6291460
  3.0 1.6 %copy-start.1 = (bf16[2048,512]{1,0:T(8,128)(2,1)S(1)}, bf16[2048,512]{1,0:T(8,128)(2,1)}, u32[]{:S(2)}) copy-start(bf16[2048,512]{1,0:T(8,128)(2,1)} %refs_5_.1) | copy-start | bytes 6291460
  4.6 0.9 copy-start.2
  5.5 0.9 copy-start.3
  6.5 0.7 copy-start.4

commit v2 on v1

--- a/solution.py
+++ b/solution.py
@@ -47,7 +47,7 @@
         return {"inp": (inp + j) % N}
 
     barrier = pltpu.get_barrier_semaphore()
-    offsets = sorted({NEAR * m for m in range(1, K)} | {1, 2, Z - 1, Z - 2})
+    offsets = (NEAR, Z - NEAR, 1, Z - 1, 2, Z - 2)
     for d in offsets:
         pl.semaphore_signal(barrier, inc=1, device_id=chip(d), device_id_type=MESH)
     for j in range(1, N):
@@ -66,6 +66,56 @@
     ]
     for q in local:
         q.start()
+
+    local[0].wait()
+    pl.semaphore_wait(barrier, len(offsets) + N + 1)
+
+    sent = []
+
+    def remote(s, d, send, recv, dev):
+        return pltpu.make_async_remote_copy(
+            src_ref=s, dst_ref=d, send_sem=send, recv_sem=recv, device_id=dev, device_id_type=MESH
+        )
+
+    def launch(*args):
+        q = remote(*args)
+        q.start()
+        sent.append(q)
+
+    two = 2 - 4 * c
+    near = (two, 1, -1)
+    arrivals = []
+    for m in range(1, K // 2 + 1):
+        arrivals += [m, -m] if m < K - m else [m]
+
+    def far_step(buf, sem, m):
+        blk = buf.at[r, c, (k - m + K) % K]
+        if 0 <= m < K // 2:
+            launch(blk, blk, sem.at[0, m + 1], sem.at[1, m + 1], chip(NEAR))
+        if -(K // 2 - 1) < m <= 0:
+            launch(blk, blk, sem.at[0, (m - 1) % K], sem.at[1, (m - 1) % K], chip(-NEAR))
+        for n, d in enumerate(near):
+            launch(blk, blk, sem.at[2 + 2 * n, m % K], sem.at[3 + 2 * n, m % K], chip(d))
+
+    def gather(buf, sem):
+        for m in arrivals:
+            got = buf.at[r, c, (k - m + K) % K]
+            remote(got, got, sem.at[0, m % K], sem.at[1, m % K], chip(NEAR)).wait_recv()
+            far_step(buf, sem, m)
+        group = buf.at[r, c]
+        launch(group, group, sem.at[8, 3], sem.at[9, 3], sib)
+        for n, d in ((1, 1), (2, -1), (0, two)):
+            s = (r - d + NEAR) % NEAR
+            for m in [0] + arrivals:
+                got = buf.at[s, c, ((z - d + Z) // NEAR - m + K) % K]
+                remote(got, got, sem.at[2 + 2 * n, m % K], sem.at[3 + 2 * n, m % K], chip(d)).wait_recv()
+            got = buf.at[s, c]
+            launch(got, got, sem.at[8, n], sem.at[9, n], sib)
+        for n, d in ((3, 0), (1, 1), (2, -1), (0, 2)):
+            got = buf.at[(r - d + NEAR) % NEAR, 1 - c]
+            remote(got, got, sem.at[8, n], sem.at[9, n], sib).wait_recv()
+
+    far_step(abuf, a_sem, 0)
 
     o = lax.broadcasted_iota(jnp.int32, (256, 256), 0)
     i = lax.broadcasted_iota(jnp.int32, (256, 256), 1)
@@ -80,41 +130,6 @@
     f0 = dot_nn(fr_t, jnp.where((row == src) & (half == 0), 1.0, 0.0).astype(BF)).astype(BF)
     f1 = dot_nn(fr_t, jnp.where((row == src) & (half == 1), 1.0, 0.0).astype(BF)).astype(BF)
 
-    local[0].wait()
-    pl.semaphore_wait(barrier, len(offsets) + N + 1)
-
-    sent = []
-
-    def remote(s, d, send, recv, dev):
-        return pltpu.make_async_remote_copy(
-            src_ref=s, dst_ref=d, send_sem=send, recv_sem=recv, device_id=dev, device_id_type=MESH
-        )
-
-    def launch(*args):
-        q = remote(*args)
-        q.start()
-        sent.append(q)
-
-    def gather(buf, sem):
-        mine = buf.at[r, c, k]
-        for m in sorted(range(1, K), key=lambda m: -min(m, K - m)):
-            launch(mine, mine, sem.at[0, m], sem.at[1, m], chip(NEAR * m))
-        for m in sorted(range(1, K), key=lambda m: min(m, K - m)):
-            got = buf.at[r, c, (k - m + K) % K]
-            remote(got, got, sem.at[0, m], sem.at[1, m], chip(NEAR * m)).wait_recv()
-        group = buf.at[r, c]
-        two = 2 - 4 * c
-        for n, d in enumerate((two, 1, -1)):
-            launch(group, group, sem.at[2, n], sem.at[3, n], chip(d))
-        launch(group, group, sem.at[4, 3], sem.at[5, 3], sib)
-        for n, d in ((1, 1), (2, -1), (0, two)):
-            got = buf.at[(r - d + NEAR) % NEAR, c]
-            remote(got, got, sem.at[2, n], sem.at[3, n], chip(d)).wait_recv()
-            launch(got, got, sem.at[4, n], sem.at[5, n], sib)
-        for n, d in ((3, 0), (1, 1), (2, -1), (0, 2)):
-            got = buf.at[(r - d + NEAR) % NEAR, 1 - c]
-            remote(got, got, sem.at[4, n], sem.at[5, n], sib).wait_recv()
-
     gather(abuf, a_sem)
 
     for j in range(K // 2):
@@ -151,7 +166,7 @@
 
     def part(start):
         w = pl.ds(pl.multiple_of(start, 512), 512)
-        return (dot_nt(gg, wg_v[w, :]) + dot_nt(ug, wu_v[w, :])).reshape(K, NEAR, 8, 512)
+        return (dot_nt(gg, wg_v[w, :]) + dot_nt(ug, wu_v[w, :])).reshape(Z, 8, 512)
 
     for h in range(2):
         sibf[h] = part((1 - c) * 1024 + h * 512)
@@ -160,43 +175,54 @@
         pown[h] = part(c * 1024 + h * 512)
     for h in range(2):
         remote(sibf.at[h], sibr.at[h], ss.at[h], sr.at[h], sib).wait_recv()
-        for s in range(NEAR):
-            both = pown[h, :, s] + sibr[h, :, s]
-            pown[h, :, s] = both
-    for s in range(NEAR):
-        csend[s] = jnp.concatenate([pown[0, :, s], pown[1, :, s]], axis=1).astype(BF)
-
-    two = 2 - 4 * c
-    for n, d in enumerate((two, 1, -1)):
-        launch(csend.at[(r + d + NEAR) % NEAR], cnear.at[n], ns.at[n], nr.at[n], chip(d))
-    acc = jnp.concatenate([pown[0, :, r], pown[1, :, r]], axis=1)
-    for n, d in ((1, 1), (2, -1), (0, two)):
-        remote(csend.at[0], cnear.at[n], ns.at[n], nr.at[n], chip(d)).wait_recv()
-        acc = acc + cnear[n].astype(F32)
-    fsend[...] = acc.astype(BF)
-    for m in sorted(range(1, K), key=lambda m: -min(m, K - m)):
-        launch(fsend.at[(k + m) % K], cfar.at[m - 1], fs.at[m], fr.at[m], chip(NEAR * m))
-    total = jnp.concatenate([pown[0, k, r], pown[1, k, r]], axis=0)
-    for n in range(3):
-        total = total + cnear[n, k].astype(F32)
+        pown[h] = pown[h] + sibr[h]
+
+    order = sorted(range(K), key=lambda m: -min(m, K - m))
+    cut = K // 2
+
+    def rows_of(w):
+        w = (w + 2 * Z) % Z
+        return jnp.concatenate([pown[0, w], pown[1, w]], axis=0)
+
+    for p in range(2):
+        part_m = pl.ds(cut * p, cut)
+        for n, d in enumerate(near):
+            for t in range(cut * p, cut * p + cut):
+                csend[n, t] = rows_of(z + d + NEAR * order[t]).astype(BF)
+            launch(csend.at[n, part_m], cnear.at[n, part_m], ns.at[n, p], nr.at[n, p], chip(d))
+    for p in range(2):
+        part_m = pl.ds(cut * p, cut)
+        for n, d in ((1, 1), (2, -1), (0, two)):
+            remote(csend.at[n, part_m], cnear.at[n, part_m], ns.at[n, p], nr.at[n, p], chip(d)).wait_recv()
+        for t in range(cut * p, cut * p + cut):
+            m = order[t]
+            total = rows_of(z + NEAR * m)
+            for n in range(3):
+                total = total + cnear[n, t].astype(F32)
+            if m:
+                fsend[m] = total.astype(BF)
+                launch(fsend.at[m], cfar.at[m], fs.at[m], fr.at[m], chip(NEAR * m))
     for m in sorted(range(1, K), key=lambda m: min(m, K - m)):
-        remote(fsend.at[0], cfar.at[m - 1], fs.at[m], fr.at[m], chip(NEAR * m)).wait_recv()
-        total = total + cfar[m - 1].astype(F32)
+        remote(fsend.at[m], cfar.at[m], fs.at[m], fr.at[m], chip(NEAR * m)).wait_recv()
+        total = total + cfar[m].astype(F32)
     dbuf[r, c, k] = total.astype(BF)
 
+    far_step(dbuf, d_sem, 0)
     gather(dbuf, d_sem)
 
+    for a in range(2):
+        x = dbuf[:, a].reshape(2 * rows, 512)
+        eloc[a, 0:20, 0:512] = dot_nn(f0, x)
+        eloc[a, 0:20, 512:1024] = dot_nn(f1, x)
+        eloc[a, 20:24, :] = jnp.zeros((4, 1024), F32)
+        launch(eloc.at[a], erem.at[a], es.at[a], er.at[a], peer)
     for a in range(2):
         blk = dbuf[r, a, k].astype(F32)
         ig_out[:, 1024 * a : 1024 * a + 512] = blk[0:8]
         ig_out[:, 1024 * a + 512 : 1024 * a + 1024] = blk[8:16]
-        x = dbuf[:, a].reshape(2 * rows, 512)
-        eloc[0:20, 1024 * a : 1024 * a + 512] = dot_nn(f0, x)
-        eloc[0:20, 1024 * a + 512 : 1024 * a + 1024] = dot_nn(f1, x)
-    eloc[20:24, :] = jnp.zeros((4, 2048), F32)
-    launch(eloc, erem, es, er, peer)
-    remote(eloc, erem, es, er, peer).wait_recv()
-    ad_out[...] = eloc[0:20, :] + erem[0:20, :]
+    for a in range(2):
+        remote(eloc.at[a], erem.at[a], es.at[a], er.at[a], peer).wait_recv()
+        ad_out[:, 1024 * a : 1024 * a + 1024] = eloc[a, 0:20, :] + erem[a, 0:20, :]
     for q in sent:
         q.wait_send()
 
@@ -224,33 +250,33 @@
             pltpu.VMEM((2048, 512), BF),
             pltpu.VMEM((2048, 512), BF),
             pltpu.VMEM((512, 2048), BF),
-            pltpu.VMEM((2, K, NEAR, 8, 512), F32),
-            pltpu.VMEM((2, K, NEAR, 8, 512), F32),
-            pltpu.VMEM((2, K, NEAR, 8, 512), F32),
-            pltpu.VMEM((NEAR, K, 16, 512), BF),
+            pltpu.VMEM((2, Z, 8, 512), F32),
+            pltpu.VMEM((2, Z, 8, 512), F32),
+            pltpu.VMEM((2, Z, 8, 512), F32),
+            pltpu.VMEM((3, K, 16, 512), BF),
             pltpu.VMEM((3, K, 16, 512), BF),
             pltpu.VMEM((K, 16, 512), BF),
-            pltpu.VMEM((K - 1, 16, 512), BF),
-            pltpu.VMEM((24, 2048), F32),
-            pltpu.VMEM((24, 2048), F32),
+            pltpu.VMEM((K, 16, 512), BF),
+            pltpu.VMEM((2, 24, 1024), F32),
+            pltpu.VMEM((2, 24, 1024), F32),
             dma((6,)),
-            dma((6, 8)),
-            dma((6, 8)),
+            dma((10, 8)),
+            dma((10, 8)),
             dma((8,)),
             dma((8,)),
             dma((8,)),
             dma((8,)),
             dma((2,)),
             dma((2,)),
-            dma((3,)),
-            dma((3,)),
-            dma((8,)),
-            dma((8,)),
-            dma,
-            dma,
+            dma((3, 2)),
+            dma((3, 2)),
+            dma((8,)),
+            dma((8,)),
+            dma((2,)),
+            dma((2,)),
         ],
         compiler_params=pltpu.CompilerParams(
-            collective_id=0, has_side_effects=True, vmem_limit_bytes=48 * 1024 * 1024
+            collective_id=0, has_side_effects=True, vmem_limit_bytes=60 * 1024 * 1024
         ),
         cost_estimate=pl.CostEstimate(flops=1_700_000_000, bytes_accessed=8_000_000, transcendentals=0),
     )(og, gate_act, up_act, frames.T, w_gate, w_up, w_down)

time: 140 us -> 131 us (0.936); the launches traced: 140 us -> 129 us
  Pallas kernels: 131 us -> 124 us
  local copies, waits for them, and re-layouts: 7.81 us -> 4.41 us
    pallas_call x1, Pallas kernels: 131 us -> 124 us  [per_device(): pl.pallas_call(functools.partial(body, Z, N), out_shape=(jax.ShapeDtypeSt...]
    unnamed x11 -> x1, local copies, waits for them, and re-layouts: 6.46 us -> 1.62 us
where the time goes in v2:
time: 131 us; the launch traced here: 129 us
  Pallas kernels  124 us (95%)
  local copies, waits for them, and re-layouts  4.41 us (3%)
    pallas_call x1, Pallas kernels, per_device(): pl.pallas_call(functools.partial(body, Z, N), out_shape=(jax.ShapeDtypeSt...  124 us

profile of v2, /device:TPU:1, one launch (start us, length us, event | category | flops | bytes accessed | tf_op | source)
XLA Modules:
  0.0 129.0 jit_solution(2009883849285956006)
XLA Ops:
  0.6 1.3 %reshape.11.refs_0_ = bf16[16,512]{1,0:T(8,128)(2,1)} reshape(bf16[4,4,512]{2,1,0:T(4,128)(2,1)} %bitcast.4) | data formatting | bytes 32768 | tf_op jit(solution)/shard_map/reshape | solution.py:232
  2.0 123.9 %shard_map.86 = (f32[8,2048]{1,0:T(8,128)}, f32[20,2048]{1,0:T(8,128)}) custom-call(bf16[16,512]{1,0:T(8,128)(2,1)} %reshape.11.refs_0_, bf16[256,512]{1,0:T(8,128)(2,1)} %refs_1_.1, bf16[256,512]{1,0:T(8,128)(2,1)} %refs_2_.1, bf16[20,256]{1,0:T(8,128)(2,1)} %bitcast.5, bf16[2048,512]{1,0:T(8,128)(2,1)} %refs_4_.1, bf16[2048,512]{1,0:T(8,128)(2,1)} %refs_5_.1, ...), custom_call_target="tpu_custom_call" | custom-call | flops 1700000000 | bytes 8000000 | tf_op jit(solution)/shard_map/pallas_call | solution.py:236
  125.9 1.5 %dynamic-slice_convert_fusion = bf16[4,2048]{1,0:T(4,128)(2,1)} fusion(f32[8,2048]{1,0:T(8,128)} %get-tuple-element.4, s32[]{:T(128)S(6)} %select_n.11), kind=kLoop, calls=%fused_computation | loop fusion | bytes 32772 | tf_op jit(solution)/shard_map/convert_element_type | solution.py:284
  127.4 1.6 %copy.11 = f32[20,2048]{1,0:T(8,128)} copy(f32[20,2048]{1,0:T(8,128)} %get-tuple-element.9) | data formatting | bytes 327680

commit v3 on v2

--- a/solution.py
+++ b/solution.py
@@ -23,7 +23,7 @@
 
 def body(Z, N, *refs):
     (og, gact, uact, frames, wg, wu, wd, ig_out, ad_out,
-     abuf, dbuf, full, hpart, hrecv, gu, gact_v, uact_v, wg_v, wu_v, wd_v,
+     abuf, dbuf, full, hpart, hsend, hrecv, hsum, gate_by, up_by, gu, gact_v, uact_v, wg_v, wu_v, wd_v,
      sibf, sibr, pown, csend, cnear, fsend, cfar, eloc, erem,
      lsem, a_sem, d_sem, hs, hr, gs, gr, ss, sr, ns, nr, fs, fr, es, er) = refs
     K = Z // NEAR
@@ -55,19 +55,20 @@
     pl.semaphore_signal(barrier, inc=1, device_id=sib, device_id_type=MESH)
     pl.semaphore_signal(barrier, inc=1, device_id=peer, device_id_type=MESH)
 
-    mine32 = pl.ds(pl.multiple_of(inp * 32, 32), 32)
     local = [
-        pltpu.make_async_copy(og, abuf.at[r, c, k], lsem.at[0]),
-        pltpu.make_async_copy(wd, wd_v, lsem.at[1]),
-        pltpu.make_async_copy(gact.at[mine32], gact_v, lsem.at[2]),
-        pltpu.make_async_copy(uact.at[mine32], uact_v, lsem.at[3]),
-        pltpu.make_async_copy(wg, wg_v, lsem.at[4]),
-        pltpu.make_async_copy(wu, wu_v, lsem.at[5]),
+        pltpu.make_async_copy(wd, wd_v, lsem.at[0]),
+        pltpu.make_async_copy(gact, gact_v, lsem.at[1]),
+        pltpu.make_async_copy(uact, uact_v, lsem.at[2]),
+        pltpu.make_async_copy(wg, wg_v, lsem.at[3]),
+        pltpu.make_async_copy(wu, wu_v, lsem.at[4]),
     ]
     for q in local:
         q.start()
 
-    local[0].wait()
+    rows4 = og[...].astype(F32)
+    abuf[r, c, k] = jnp.concatenate(
+        [rows4[:, 512 * q : 512 * q + 512] for q in range(4)], axis=0
+    ).astype(BF)
     pl.semaphore_wait(barrier, len(offsets) + N + 1)
 
     sent = []
@@ -84,29 +85,31 @@
 
     two = 2 - 4 * c
     near = (two, 1, -1)
-    arrivals = []
-    for m in range(1, K // 2 + 1):
-        arrivals += [m, -m] if m < K - m else [m]
-
-    def far_step(buf, sem, m):
+    arrivals = (1, -1, 2, -2, 3, -3, 4)
+    early = {1: (0, 0, 1), -1: (0, 0, -1), 2: (1, 1, 1), -2: (-1, -1, -1),
+             3: (-1, 1, 2), -3: (-1, -1, -2), 4: (2, 2, 2)}
+    late = {4: (0, 0, 4), 1: (0, 0, 1), -1: (0, 0, -1), 2: (1, 1, 1), -2: (-1, -1, -1),
+            3: (2, 2, 1), -3: (-2, -2, -1)}
+
+    def far_step(buf, sem, tree, m):
+        for to, (after, held, step) in tree.items():
+            if after == m:
+                blk = buf.at[r, c, (k - held + K) % K]
+                launch(blk, blk, sem.at[0, to % K], sem.at[1, to % K], chip(NEAR * step))
         blk = buf.at[r, c, (k - m + K) % K]
-        if 0 <= m < K // 2:
-            launch(blk, blk, sem.at[0, m + 1], sem.at[1, m + 1], chip(NEAR))
-        if -(K // 2 - 1) < m <= 0:
-            launch(blk, blk, sem.at[0, (m - 1) % K], sem.at[1, (m - 1) % K], chip(-NEAR))
         for n, d in enumerate(near):
             launch(blk, blk, sem.at[2 + 2 * n, m % K], sem.at[3 + 2 * n, m % K], chip(d))
 
-    def gather(buf, sem):
+    def gather(buf, sem, tree):
         for m in arrivals:
             got = buf.at[r, c, (k - m + K) % K]
             remote(got, got, sem.at[0, m % K], sem.at[1, m % K], chip(NEAR)).wait_recv()
-            far_step(buf, sem, m)
+            far_step(buf, sem, tree, m)
         group = buf.at[r, c]
         launch(group, group, sem.at[8, 3], sem.at[9, 3], sib)
         for n, d in ((1, 1), (2, -1), (0, two)):
             s = (r - d + NEAR) % NEAR
-            for m in [0] + arrivals:
+            for m in (0,) + arrivals:
                 got = buf.at[s, c, ((z - d + Z) // NEAR - m + K) % K]
                 remote(got, got, sem.at[2 + 2 * n, m % K], sem.at[3 + 2 * n, m % K], chip(d)).wait_recv()
             got = buf.at[s, c]
@@ -115,7 +118,7 @@
             got = buf.at[(r - d + NEAR) % NEAR, 1 - c]
             remote(got, got, sem.at[8, n], sem.at[9, n], sib).wait_recv()
 
-    far_step(abuf, a_sem, 0)
+    far_step(abuf, a_sem, early, 0)
 
     o = lax.broadcasted_iota(jnp.int32, (256, 256), 0)
     i = lax.broadcasted_iota(jnp.int32, (256, 256), 1)
@@ -130,39 +133,52 @@
     f0 = dot_nn(fr_t, jnp.where((row == src) & (half == 0), 1.0, 0.0).astype(BF)).astype(BF)
     f1 = dot_nn(fr_t, jnp.where((row == src) & (half == 1), 1.0, 0.0).astype(BF)).astype(BF)
 
-    gather(abuf, a_sem)
+    local[1].wait()
+    local[2].wait()
+    for t in range(N):
+        part32 = pl.ds(32 * t, 32)
+        gate = gact_v[part32].astype(F32)
+        upper = uact_v[part32].astype(F32)
+        sigma = jax.nn.sigmoid(gate)
+        gate_by[t] = upper * sigma * (1.0 + gate * (1.0 - sigma))
+        up_by[t] = gate * sigma
+    gather(abuf, a_sem, early)
 
     for j in range(K // 2):
         rows_in = abuf[:, :, 2 * j : 2 * j + 2].reshape(256, 512)
         out = dot_nn(perm, rows_in).astype(BF)
         for q in range(4):
             full[64 * j : 64 * j + 64, 512 * q : 512 * q + 512] = out[64 * q : 64 * q + 64]
-    local[1].wait()
+    local[0].wait()
     hpart[...] = dot_nt(full[...], wd_v[...]).reshape(hpart.shape)
-
-    for j in range(1, N):
-        launch(hpart.at[(inp + j) % N], hrecv.at[j - 1], hs.at[j], hr.at[j], ring(j))
-    local[2].wait()
+    hsend[...] = hpart[...].astype(BF)
+
+    for j in range(1, N):
+        launch(hsend.at[(inp + j) % N], hrecv.at[j - 1], hs.at[j], hr.at[j], ring(j))
+    total = hpart[inp]
+    for j in range(1, N):
+        remote(hsend.at[inp], hrecv.at[j - 1], hs.at[j], hr.at[j], ring(j)).wait_recv()
+        total = total + hrecv[j - 1].astype(F32)
+    hsum[inp] = total.astype(BF)
+    for j in range(1, N):
+        launch(hsum.at[inp], hsum.at[inp], gs.at[j], gr.at[j], ring(j))
+
+    def grads(t):
+        h = hsum[t].astype(F32)
+        gu[0, t] = (h * gate_by[t]).astype(BF)
+        gu[1, t] = (h * up_by[t]).astype(BF)
+
+    grads(inp)
     local[3].wait()
-    gate = gact_v[...].astype(F32)
-    upper = uact_v[...].astype(F32)
-    sigma = jax.nn.sigmoid(gate)
-    total = hpart[inp]
-    for j in range(1, N):
-        remote(hpart.at[(inp + j) % N], hrecv.at[j - 1], hs.at[j], hr.at[j], ring(j)).wait_recv()
-        total = total + hrecv[j - 1]
-    gu[inp, 0] = (total * upper * sigma * (1.0 + gate * (1.0 - sigma))).astype(BF)
-    gu[inp, 1] = (total * gate * sigma).astype(BF)
-    for j in range(1, N):
-        launch(gu.at[inp], gu.at[inp], gs.at[j], gr.at[j], ring(j))
     local[4].wait()
-    local[5].wait()
-    for j in range(1, N):
-        got = gu.at[(inp - j + N) % N]
+    for j in range(1, N):
+        t = (inp - j + N) % N
+        got = hsum.at[t]
         remote(got, got, gs.at[j], gr.at[j], ring(j)).wait_recv()
-
-    gg = gu[:, 0].reshape(256, 512)
-    ug = gu[:, 1].reshape(256, 512)
+        grads(t)
+
+    gg = gu[0].reshape(256, 512)
+    ug = gu[1].reshape(256, 512)
 
     def part(start):
         w = pl.ds(pl.multiple_of(start, 512), 512)
@@ -207,8 +223,8 @@
         total = total + cfar[m].astype(F32)
     dbuf[r, c, k] = total.astype(BF)
 
-    far_step(dbuf, d_sem, 0)
-    gather(dbuf, d_sem)
+    far_step(dbuf, d_sem, late, 0)
+    gather(dbuf, d_sem, late)
 
     for a in range(2):
         x = dbuf[:, a].reshape(2 * rows, 512)
@@ -218,8 +234,10 @@
         launch(eloc.at[a], erem.at[a], es.at[a], er.at[a], peer)
     for a in range(2):
         blk = dbuf[r, a, k].astype(F32)
-        ig_out[:, 1024 * a : 1024 * a + 512] = blk[0:8]
-        ig_out[:, 1024 * a + 512 : 1024 * a + 1024] = blk[8:16]
+        for h in range(2):
+            block8 = blk[8 * h : 8 * h + 8]
+            at = 1024 * a + 512 * h
+            ig_out[:, at : at + 512] = jnp.where(c == 0, block8[0:4], block8[4:8])
     for a in range(2):
         remote(eloc.at[a], erem.at[a], es.at[a], er.at[a], peer).wait_recv()
         ad_out[:, 1024 * a : 1024 * a + 1024] = eloc[a, 0:20, :] + erem[a, 0:20, :]
@@ -227,26 +245,34 @@
         q.wait_send()
 
 
+def finish(ig, ad, ig_out, ad_out):
+    ig_out[...] = ig[...].astype(BF)
+    ad_out[...] = ad[...]
+
+
 def per_device(Z, N, out_grad, gate_act, up_act, frames, w_gate, w_up, w_down):
     K = Z // NEAR
-    og = out_grad.reshape(4, 4, 512).transpose(1, 0, 2).reshape(16, 512)
     hbm = pl.BlockSpec(memory_space=pl.ANY)
     vmem = pl.BlockSpec(memory_space=pltpu.VMEM)
     dma = pltpu.SemaphoreType.DMA
-    ig8, ad = pl.pallas_call(
+    ig, ad = pl.pallas_call(
         functools.partial(body, Z, N),
-        out_shape=(jax.ShapeDtypeStruct((8, 2048), F32), jax.ShapeDtypeStruct((20, 2048), F32)),
-        in_specs=[hbm, hbm, hbm, vmem, hbm, hbm, hbm],
+        out_shape=(jax.ShapeDtypeStruct((4, 2048), F32), jax.ShapeDtypeStruct((20, 2048), F32)),
+        in_specs=[vmem, hbm, hbm, vmem, hbm, hbm, hbm],
         out_specs=(vmem, vmem),
         scratch_shapes=[
             pltpu.VMEM((NEAR, 2, K, 16, 512), BF),
             pltpu.VMEM((NEAR, 2, K, 16, 512), BF),
             pltpu.VMEM((256, 2048), BF),
             pltpu.VMEM((N, 32, 512), F32),
-            pltpu.VMEM((N - 1, 32, 512), F32),
-            pltpu.VMEM((N, 2, 32, 512), BF),
-            pltpu.VMEM((32, 512), BF),
-            pltpu.VMEM((32, 512), BF),
+            pltpu.VMEM((N, 32, 512), BF),
+            pltpu.VMEM((N - 1, 32, 512), BF),
+            pltpu.VMEM((N, 32, 512), BF),
+            pltpu.VMEM((N, 32, 512), F32),
+            pltpu.VMEM((N, 32, 512), F32),
+            pltpu.VMEM((2, N, 32, 512), BF),
+            pltpu.VMEM((256, 512), BF),
+            pltpu.VMEM((256, 512), BF),
             pltpu.VMEM((2048, 512), BF),
             pltpu.VMEM((2048, 512), BF),
             pltpu.VMEM((512, 2048), BF),
@@ -259,7 +285,7 @@
             pltpu.VMEM((K, 16, 512), BF),
             pltpu.VMEM((2, 24, 1024), F32),
             pltpu.VMEM((2, 24, 1024), F32),
-            dma((6,)),
+            dma((5,)),
             dma((10, 8)),
             dma((10, 8)),
             dma((8,)),
@@ -279,10 +305,14 @@
             collective_id=0, has_side_effects=True, vmem_limit_bytes=60 * 1024 * 1024
         ),
         cost_estimate=pl.CostEstimate(flops=1_700_000_000, bytes_accessed=8_000_000, transcendentals=0),
-    )(og, gate_act, up_act, frames.T, w_gate, w_up, w_down)
-    core = lax.axis_index("hid") % 2
-    input_grad = lax.dynamic_slice_in_dim(ig8, core * 4, 4, 0).astype(BF)
-    return input_grad, ad
+    )(out_grad, gate_act, up_act, frames.T, w_gate, w_up, w_down)
+    return pl.pallas_call(
+        finish,
+        out_shape=(jax.ShapeDtypeStruct((4, 2048), BF), jax.ShapeDtypeStruct((20, 2048), F32)),
+        in_specs=[vmem, vmem],
+        out_specs=(vmem, vmem),
+        compiler_params=pltpu.CompilerParams(vmem_limit_bytes=60 * 1024 * 1024),
+    )(ig, ad)
 
 
 def solution(mesh):

time: 131 us -> 120 us (0.916)
  Pallas kernels: 124 us -> 119 us
  local copies, waits for them, and re-layouts: 4.41 us -> 0 us
    pallas_call x1, Pallas kernels: 124 us -> 117 us  [per_device(): pl.pallas_call(functools.partial(body, Z, N), out_shape=(jax.ShapeDtypeSt...]
    pallas_call x0 -> x1, Pallas kernels: none -> 1.65 us  [per_device(): pl.pallas_call(finish, out_shape=(jax.ShapeDtypeStruct((4, 2048), BF), ja...]
    unnamed x1 -> x0, local copies, waits for them, and re-layouts: 1.62 us -> none
    convert_element_type x1 -> x0, local copies, waits for them, and re-layouts: 1.46 us -> none  [per_device(): input_grad = lax.dynamic_slice_in_dim(ig8, core * 4, 4, 0).astype(BF)]
    reshape x1 -> x0, local copies, waits for them, and re-layouts: 1.33 us -> none  [per_device(): og = out_grad.reshape(4, 4, 512).transpose(1, 0, 2).reshape(16, 512)]
where the time goes in v3:
time: 120 us; the launch traced here: 119 us
  Pallas kernels  119 us (99%)
    pallas_call x1, Pallas kernels, per_device(): pl.pallas_call(functools.partial(body, Z, N), out_shape=(jax.ShapeDtypeSt...  117 us

profile of v3, /device:TPU:1, one launch (start us, length us, event | category | flops | bytes accessed | tf_op | source)
XLA Modules:
  0.0 119.3 jit_solution(7840475381198844243)
XLA Ops:
  0.6 117.0 %shard_map.86 = (f32[4,2048]{1,0:T(4,128)}, f32[20,2048]{1,0:T(8,128)}) custom-call(bf16[4,2048]{1,0:T(4,128)(2,1)} %refs_0_.1, bf16[256,512]{1,0:T(8,128)(2,1)} %refs_1_.1, bf16[256,512]{1,0:T(8,128)(2,1)} %refs_2_.1, bf16[20,256]{1,0:T(8,128)(2,1)} %bitcast.1, bf16[2048,512]{1,0:T(8,128)(2,1)} %refs_4_.1, bf16[2048,512]{1,0:T(8,128)(2,1)} %refs_5_.1, ...), custom_call_target="tpu_custom_call" | custom-call | flops 1700000000 | bytes 8000000 | tf_op jit(solution)/shard_map/pallas_call | solution.py:258
  117.7 1.6 %shard_map.87 = (bf16[4,2048]{1,0:T(4,128)(2,1)}, f32[20,2048]{1,0:T(8,128)}) custom-call(f32[4,2048]{1,0:T(4,128)} %get-tuple-element.4.ig, f32[20,2048]{1,0:T(8,128)} %get-tuple-element.5.ad), custom_call_target="tpu_custom_call" | custom-call | tf_op jit(solution)/shard_map/pallas_call | solution.py:309

commit v4 on v3

--- a/solution.py
+++ b/solution.py
@@ -100,20 +100,25 @@
         for n, d in enumerate(near):
             launch(blk, blk, sem.at[2 + 2 * n, m % K], sem.at[3 + 2 * n, m % K], chip(d))
 
-    def gather(buf, sem, tree):
+    def gather(*chains):
         for m in arrivals:
-            got = buf.at[r, c, (k - m + K) % K]
-            remote(got, got, sem.at[0, m % K], sem.at[1, m % K], chip(NEAR)).wait_recv()
-            far_step(buf, sem, tree, m)
-        group = buf.at[r, c]
-        launch(group, group, sem.at[8, 3], sem.at[9, 3], sib)
+            for buf, sem, tree in chains:
+                got = buf.at[r, c, (k - m + K) % K]
+                remote(got, got, sem.at[0, m % K], sem.at[1, m % K], chip(NEAR)).wait_recv()
+                far_step(buf, sem, tree, m)
+        for buf, sem, tree in chains:
+            group = buf.at[r, c]
+            launch(group, group, sem.at[8, 3], sem.at[9, 3], sib)
         for n, d in ((1, 1), (2, -1), (0, two)):
             s = (r - d + NEAR) % NEAR
-            for m in (0,) + arrivals:
-                got = buf.at[s, c, ((z - d + Z) // NEAR - m + K) % K]
-                remote(got, got, sem.at[2 + 2 * n, m % K], sem.at[3 + 2 * n, m % K], chip(d)).wait_recv()
-            got = buf.at[s, c]
-            launch(got, got, sem.at[8, n], sem.at[9, n], sib)
+            for buf, sem, tree in chains:
+                for m in (0,) + arrivals:
+                    got = buf.at[s, c, ((z - d + Z) // NEAR - m + K) % K]
+                    remote(got, got, sem.at[2 + 2 * n, m % K], sem.at[3 + 2 * n, m % K], chip(d)).wait_recv()
+                got = buf.at[s, c]
+                launch(got, got, sem.at[8, n], sem.at[9, n], sib)
+
+    def from_other_core(buf, sem):
         for n, d in ((3, 0), (1, 1), (2, -1), (0, 2)):
             got = buf.at[(r - d + NEAR) % NEAR, 1 - c]
             remote(got, got, sem.at[8, n], sem.at[9, n], sib).wait_recv()
@@ -142,7 +147,8 @@
         sigma = jax.nn.sigmoid(gate)
         gate_by[t] = upper * sigma * (1.0 + gate * (1.0 - sigma))
         up_by[t] = gate * sigma
-    gather(abuf, a_sem, early)
+    gather((abuf, a_sem, early))
+    from_other_core(abuf, a_sem)
 
     for j in range(K // 2):
         rows_in = abuf[:, :, 2 * j : 2 * j + 2].reshape(256, 512)
@@ -184,63 +190,66 @@
         w = pl.ds(pl.multiple_of(start, 512), 512)
         return (dot_nt(gg, wg_v[w, :]) + dot_nt(ug, wu_v[w, :])).reshape(Z, 8, 512)
 
+    order = sorted(range(K), key=lambda m: -min(m, K - m))
+
+    def rows_of(h, w):
+        own = pown[h, (w + 2 * Z) % Z]
+        return jnp.concatenate([own[:, 0:256], own[:, 256:512]], axis=0)
+
     for h in range(2):
         sibf[h] = part((1 - c) * 1024 + h * 512)
         launch(sibf.at[h], sibr.at[h], ss.at[h], sr.at[h], sib)
-    for h in range(2):
         pown[h] = part(c * 1024 + h * 512)
-    for h in range(2):
         remote(sibf.at[h], sibr.at[h], ss.at[h], sr.at[h], sib).wait_recv()
         pown[h] = pown[h] + sibr[h]
-
-    order = sorted(range(K), key=lambda m: -min(m, K - m))
-    cut = K // 2
-
-    def rows_of(w):
-        w = (w + 2 * Z) % Z
-        return jnp.concatenate([pown[0, w], pown[1, w]], axis=0)
-
-    for p in range(2):
-        part_m = pl.ds(cut * p, cut)
         for n, d in enumerate(near):
-            for t in range(cut * p, cut * p + cut):
-                csend[n, t] = rows_of(z + d + NEAR * order[t]).astype(BF)
-            launch(csend.at[n, part_m], cnear.at[n, part_m], ns.at[n, p], nr.at[n, p], chip(d))
-    for p in range(2):
-        part_m = pl.ds(cut * p, cut)
+            for t in range(K):
+                csend[h, n, t] = rows_of(h, z + d + NEAR * order[t]).astype(BF)
+            launch(csend.at[h, n], cnear.at[h, n], ns.at[h, n], nr.at[h, n], chip(d))
+    last = [None, None]
+    for h in range(2):
         for n, d in ((1, 1), (2, -1), (0, two)):
-            remote(csend.at[n, part_m], cnear.at[n, part_m], ns.at[n, p], nr.at[n, p], chip(d)).wait_recv()
-        for t in range(cut * p, cut * p + cut):
+            remote(csend.at[h, n], cnear.at[h, n], ns.at[h, n], nr.at[h, n], chip(d)).wait_recv()
+        for t in range(K):
             m = order[t]
-            total = rows_of(z + NEAR * m)
+            total = rows_of(h, z + NEAR * m)
             for n in range(3):
-                total = total + cnear[n, t].astype(F32)
+                total = total + cnear[h, n, t].astype(F32)
             if m:
-                fsend[m] = total.astype(BF)
-                launch(fsend.at[m], cfar.at[m], fs.at[m], fr.at[m], chip(NEAR * m))
-    for m in sorted(range(1, K), key=lambda m: min(m, K - m)):
-        remote(fsend.at[m], cfar.at[m], fs.at[m], fr.at[m], chip(NEAR * m)).wait_recv()
-        total = total + cfar[m].astype(F32)
-    dbuf[r, c, k] = total.astype(BF)
-
-    far_step(dbuf, d_sem, late, 0)
-    gather(dbuf, d_sem, late)
-
-    for a in range(2):
-        x = dbuf[:, a].reshape(2 * rows, 512)
-        eloc[a, 0:20, 0:512] = dot_nn(f0, x)
-        eloc[a, 0:20, 512:1024] = dot_nn(f1, x)
-        eloc[a, 20:24, :] = jnp.zeros((4, 1024), F32)
-        launch(eloc.at[a], erem.at[a], es.at[a], er.at[a], peer)
-    for a in range(2):
-        blk = dbuf[r, a, k].astype(F32)
-        for h in range(2):
-            block8 = blk[8 * h : 8 * h + 8]
+                fsend[h, m] = total.astype(BF)
+                launch(fsend.at[h, m], cfar.at[h, m], fs.at[h, m], fr.at[h, m], chip(NEAR * m))
+        last[h] = total
+    for h in range(2):
+        total = last[h]
+        for m in sorted(range(1, K), key=lambda m: min(m, K - m)):
+            remote(fsend.at[h, m], cfar.at[h, m], fs.at[h, m], fr.at[h, m], chip(NEAR * m)).wait_recv()
+            total = total + cfar[h, m].astype(F32)
+        dbuf[h, r, c, k] = total.astype(BF)
+        far_step(dbuf.at[h], d_sem.at[h], late, 0)
+
+    gather(*((dbuf.at[h], d_sem.at[h], late) for h in range(2)))
+
+    for h in range(2):
+        from_other_core(dbuf.at[h], d_sem.at[h])
+        for a in range(2):
+            x = dbuf[h, :, a].reshape(2 * rows, 256)
+            eloc[h, 0:20, 512 * a : 512 * a + 256] = dot_nn(f0, x)
+            eloc[h, 0:20, 512 * a + 256 : 512 * a + 512] = dot_nn(f1, x)
+        eloc[h, 20:24, :] = jnp.zeros((4, 1024), F32)
+        launch(eloc.at[h], erem.at[h], es.at[h], er.at[h], peer)
+    for h in range(2):
+        for a in range(2):
+            blk = dbuf[h, r, a, k].astype(F32)
+            for e in range(2):
+                block8 = blk[8 * e : 8 * e + 8]
+                at = 1024 * a + 512 * h + 256 * e
+                ig_out[:, at : at + 256] = jnp.where(c == 0, block8[0:4], block8[4:8])
+    for h in range(2):
+        remote(eloc.at[h], erem.at[h], es.at[h], er.at[h], peer).wait_recv()
+        for a in range(2):
             at = 1024 * a + 512 * h
-            ig_out[:, at : at + 512] = jnp.where(c == 0, block8[0:4], block8[4:8])
-    for a in range(2):
-        remote(eloc.at[a], erem.at[a], es.at[a], er.at[a], peer).wait_recv()
-        ad_out[:, 1024 * a : 1024 * a + 1024] = eloc[a, 0:20, :] + erem[a, 0:20, :]
+            cols = pl.ds(512 * a, 512)
+            ad_out[:, at : at + 512] = eloc[h, 0:20, cols] + erem[h, 0:20, cols]
     for q in sent:
         q.wait_send()
 
@@ -262,7 +271,7 @@
         out_specs=(vmem, vmem),
         scratch_shapes=[
             pltpu.VMEM((NEAR, 2, K, 16, 512), BF),
-            pltpu.VMEM((NEAR, 2, K, 16, 512), BF),
+            pltpu.VMEM((2, NEAR, 2, K, 16, 256), BF),
             pltpu.VMEM((256, 2048), BF),
             pltpu.VMEM((N, 32, 512), F32),
             pltpu.VMEM((N, 32, 512), BF),
@@ -279,25 +288,25 @@
             pltpu.VMEM((2, Z, 8, 512), F32),
             pltpu.VMEM((2, Z, 8, 512), F32),
             pltpu.VMEM((2, Z, 8, 512), F32),
-            pltpu.VMEM((3, K, 16, 512), BF),
-            pltpu.VMEM((3, K, 16, 512), BF),
-            pltpu.VMEM((K, 16, 512), BF),
-            pltpu.VMEM((K, 16, 512), BF),
+            pltpu.VMEM((2, 3, K, 16, 256), BF),
+            pltpu.VMEM((2, 3, K, 16, 256), BF),
+            pltpu.VMEM((2, K, 16, 256), BF),
+            pltpu.VMEM((2, K, 16, 256), BF),
             pltpu.VMEM((2, 24, 1024), F32),
             pltpu.VMEM((2, 24, 1024), F32),
             dma((5,)),
             dma((10, 8)),
-            dma((10, 8)),
+            dma((2, 10, 8)),
             dma((8,)),
             dma((8,)),
             dma((8,)),
             dma((8,)),
             dma((2,)),
             dma((2,)),
-            dma((3, 2)),
-            dma((3, 2)),
-            dma((8,)),
-            dma((8,)),
+            dma((2, 3)),
+            dma((2, 3)),
+            dma((2, 8)),
+            dma((2, 8)),
             dma((2,)),
             dma((2,)),
         ],

time: 120 us -> 120 us (level)
  no operation moved by 1% of the time
where the time goes in v4:
time: 120 us
  Pallas kernels  119 us (99%)
    pallas_call x1, Pallas kernels, per_device(): pl.pallas_call(functools.partial(body, Z, N), out_shape=(jax.ShapeDtypeSt...  117 us

profile of v4, /device:TPU:1, one launch (start us, length us, event | category | flops | bytes accessed | tf_op | source)
XLA Modules:
  0.0 119.7 jit_solution(17538082443365051606)
XLA Ops:
  0.6 117.4 %shard_map.86 = (f32[4,2048]{1,0:T(4,128)}, f32[20,2048]{1,0:T(8,128)}) custom-call(bf16[4,2048]{1,0:T(4,128)(2,1)} %refs_0_.1, bf16[256,512]{1,0:T(8,128)(2,1)} %refs_1_.1, bf16[256,512]{1,0:T(8,128)(2,1)} %refs_2_.1, bf16[20,256]{1,0:T(8,128)(2,1)} %bitcast.1, bf16[2048,512]{1,0:T(8,128)(2,1)} %refs_4_.1, bf16[2048,512]{1,0:T(8,128)(2,1)} %refs_5_.1, ...), custom_call_target="tpu_custom_call" | custom-call | flops 1700000000 | bytes 8000000 | tf_op jit(solution)/shard_map/pallas_call | solution.py:267
  118.1 1.6 %shard_map.87 = (bf16[4,2048]{1,0:T(4,128)(2,1)}, f32[20,2048]{1,0:T(8,128)}) custom-call(f32[4,2048]{1,0:T(4,128)} %get-tuple-element.4.ig, f32[20,2048]{1,0:T(8,128)} %get-tuple-element.5.ad), custom_call_target="tpu_custom_call" | custom-call | tf_op jit(solution)/shard_map/pallas_call | solution.py:318

commit v5 on v3

--- a/solution.py
+++ b/solution.py
@@ -71,17 +71,19 @@
     ).astype(BF)
     pl.semaphore_wait(barrier, len(offsets) + N + 1)
 
-    sent = []
-
     def remote(s, d, send, recv, dev):
         return pltpu.make_async_remote_copy(
             src_ref=s, dst_ref=d, send_sem=send, recv_sem=recv, device_id=dev, device_id_type=MESH
         )
 
     def launch(*args):
-        q = remote(*args)
-        q.start()
-        sent.append(q)
+        remote(*args).start()
+
+    def wait_sent(ref, sem):
+        remote(ref, ref, sem, sem, sib).wait_send()
+
+    def wait_received(ref, sem):
+        remote(ref, ref, sem, sem, sib).wait_recv()
 
     two = 2 - 4 * c
     near = (two, 1, -1)
@@ -95,28 +97,29 @@
         for to, (after, held, step) in tree.items():
             if after == m:
                 blk = buf.at[r, c, (k - held + K) % K]
-                launch(blk, blk, sem.at[0, to % K], sem.at[1, to % K], chip(NEAR * step))
+                launch(blk, blk, sem.at[0], sem.at[10 + to % K], chip(NEAR * step))
         blk = buf.at[r, c, (k - m + K) % K]
         for n, d in enumerate(near):
-            launch(blk, blk, sem.at[2 + 2 * n, m % K], sem.at[3 + 2 * n, m % K], chip(d))
+            launch(blk, blk, sem.at[1], sem.at[3 + n], chip(d))
 
     def gather(buf, sem, tree):
         for m in arrivals:
-            got = buf.at[r, c, (k - m + K) % K]
-            remote(got, got, sem.at[0, m % K], sem.at[1, m % K], chip(NEAR)).wait_recv()
+            wait_received(buf.at[r, c, (k - m + K) % K], sem.at[10 + m % K])
             far_step(buf, sem, tree, m)
         group = buf.at[r, c]
-        launch(group, group, sem.at[8, 3], sem.at[9, 3], sib)
+        launch(group, group, sem.at[2], sem.at[9], sib)
         for n, d in ((1, 1), (2, -1), (0, two)):
-            s = (r - d + NEAR) % NEAR
-            for m in (0,) + arrivals:
-                got = buf.at[s, c, ((z - d + Z) // NEAR - m + K) % K]
-                remote(got, got, sem.at[2 + 2 * n, m % K], sem.at[3 + 2 * n, m % K], chip(d)).wait_recv()
-            got = buf.at[s, c]
-            launch(got, got, sem.at[8, n], sem.at[9, n], sib)
+            got = buf.at[(r - d + NEAR) % NEAR, c]
+            wait_received(got, sem.at[3 + n])
+            launch(got, got, sem.at[2], sem.at[6 + n], sib)
+
+    def from_other_core(buf, sem):
         for n, d in ((3, 0), (1, 1), (2, -1), (0, 2)):
-            got = buf.at[(r - d + NEAR) % NEAR, 1 - c]
-            remote(got, got, sem.at[8, n], sem.at[9, n], sib).wait_recv()
+            wait_received(buf.at[(r - d + NEAR) % NEAR, 1 - c], sem.at[6 + n])
+
+    def gather_sent(buf, sem):
+        wait_sent(buf.at[0, 0, pl.ds(0, K - 1)], sem.at[0])
+        wait_sent(buf.at[pl.ds(0, 3), 0], sem.at[1])
 
     far_step(abuf, a_sem, early, 0)
 
@@ -143,6 +146,7 @@
         gate_by[t] = upper * sigma * (1.0 + gate * (1.0 - sigma))
         up_by[t] = gate * sigma
     gather(abuf, a_sem, early)
+    from_other_core(abuf, a_sem)
 
     for j in range(K // 2):
         rows_in = abuf[:, :, 2 * j : 2 * j + 2].reshape(256, 512)
@@ -154,14 +158,14 @@
     hsend[...] = hpart[...].astype(BF)
 
     for j in range(1, N):
-        launch(hsend.at[(inp + j) % N], hrecv.at[j - 1], hs.at[j], hr.at[j], ring(j))
+        launch(hsend.at[(inp + j) % N], hrecv.at[j - 1], hs, hr, ring(j))
     total = hpart[inp]
-    for j in range(1, N):
-        remote(hsend.at[inp], hrecv.at[j - 1], hs.at[j], hr.at[j], ring(j)).wait_recv()
+    wait_received(hrecv, hr)
+    for j in range(1, N):
         total = total + hrecv[j - 1].astype(F32)
     hsum[inp] = total.astype(BF)
     for j in range(1, N):
-        launch(hsum.at[inp], hsum.at[inp], gs.at[j], gr.at[j], ring(j))
+        launch(hsum.at[inp], hsum.at[inp], gs, gr, ring(j))
 
     def grads(t):
         h = hsum[t].astype(F32)
@@ -171,11 +175,9 @@
     grads(inp)
     local[3].wait()
     local[4].wait()
-    for j in range(1, N):
-        t = (inp - j + N) % N
-        got = hsum.at[t]
-        remote(got, got, gs.at[j], gr.at[j], ring(j)).wait_recv()
-        grads(t)
+    wait_received(hsum.at[pl.ds(0, N - 1)], gr)
+    for j in range(1, N):
+        grads((inp - j + N) % N)
 
     gg = gu[0].reshape(256, 512)
     ug = gu[1].reshape(256, 512)
@@ -186,11 +188,11 @@
 
     for h in range(2):
         sibf[h] = part((1 - c) * 1024 + h * 512)
-        launch(sibf.at[h], sibr.at[h], ss.at[h], sr.at[h], sib)
+        launch(sibf.at[h], sibr.at[h], ss, sr.at[h], sib)
     for h in range(2):
         pown[h] = part(c * 1024 + h * 512)
     for h in range(2):
-        remote(sibf.at[h], sibr.at[h], ss.at[h], sr.at[h], sib).wait_recv()
+        wait_received(sibr.at[h], sr.at[h])
         pown[h] = pown[h] + sibr[h]
 
     order = sorted(range(K), key=lambda m: -min(m, K - m))
@@ -205,11 +207,11 @@
         for n, d in enumerate(near):
             for t in range(cut * p, cut * p + cut):
                 csend[n, t] = rows_of(z + d + NEAR * order[t]).astype(BF)
-            launch(csend.at[n, part_m], cnear.at[n, part_m], ns.at[n, p], nr.at[n, p], chip(d))
+            launch(csend.at[n, part_m], cnear.at[n, part_m], ns, nr.at[n, p], chip(d))
     for p in range(2):
         part_m = pl.ds(cut * p, cut)
         for n, d in ((1, 1), (2, -1), (0, two)):
-            remote(csend.at[n, part_m], cnear.at[n, part_m], ns.at[n, p], nr.at[n, p], chip(d)).wait_recv()
+            wait_received(cnear.at[n, part_m], nr.at[n, p])
         for t in range(cut * p, cut * p + cut):
             m = order[t]
             total = rows_of(z + NEAR * m)
@@ -217,32 +219,45 @@
                 total = total + cnear[n, t].astype(F32)
             if m:
                 fsend[m] = total.astype(BF)
-                launch(fsend.at[m], cfar.at[m], fs.at[m], fr.at[m], chip(NEAR * m))
-    for m in sorted(range(1, K), key=lambda m: min(m, K - m)):
-        remote(fsend.at[m], cfar.at[m], fs.at[m], fr.at[m], chip(NEAR * m)).wait_recv()
+                launch(fsend.at[m], cfar.at[m], fs, fr, chip(NEAR * m))
+    others = pl.ds(1, K - 1)
+    wait_received(cfar.at[others], fr)
+    for m in range(1, K):
         total = total + cfar[m].astype(F32)
     dbuf[r, c, k] = total.astype(BF)
 
     far_step(dbuf, d_sem, late, 0)
+    gather_sent(abuf, a_sem)
+    wait_sent(abuf.at[:, 0], a_sem.at[2])
+    wait_sent(hsend.at[pl.ds(0, N - 1)], hs)
+    wait_sent(hsum.at[pl.ds(0, N - 1)], gs)
+    wait_sent(sibf, ss)
+    wait_sent(csend, ns)
+    wait_sent(fsend.at[others], fs)
     gather(dbuf, d_sem, late)
 
-    for a in range(2):
+    def adapter_part(a):
         x = dbuf[:, a].reshape(2 * rows, 512)
         eloc[a, 0:20, 0:512] = dot_nn(f0, x)
         eloc[a, 0:20, 512:1024] = dot_nn(f1, x)
-        eloc[a, 20:24, :] = jnp.zeros((4, 1024), F32)
-        launch(eloc.at[a], erem.at[a], es.at[a], er.at[a], peer)
+        launch(eloc.at[a], erem.at[a], es, er.at[a], peer)
+
+    eloc[:, 20:24, :] = jnp.zeros((2, 4, 1024), F32)
+    adapter_part(c)
+    gather_sent(dbuf, d_sem)
+    from_other_core(dbuf, d_sem)
+    adapter_part(1 - c)
     for a in range(2):
         blk = dbuf[r, a, k].astype(F32)
         for h in range(2):
             block8 = blk[8 * h : 8 * h + 8]
             at = 1024 * a + 512 * h
             ig_out[:, at : at + 512] = jnp.where(c == 0, block8[0:4], block8[4:8])
+    wait_sent(dbuf.at[:, 0], d_sem.at[2])
     for a in range(2):
-        remote(eloc.at[a], erem.at[a], es.at[a], er.at[a], peer).wait_recv()
+        wait_received(erem.at[a], er.at[a])
         ad_out[:, 1024 * a : 1024 * a + 1024] = eloc[a, 0:20, :] + erem[a, 0:20, :]
-    for q in sent:
-        q.wait_send()
+    wait_sent(eloc, es)
 
 
 def finish(ig, ad, ig_out, ad_out):
@@ -286,19 +301,19 @@
             pltpu.VMEM((2, 24, 1024), F32),
             pltpu.VMEM((2, 24, 1024), F32),
             dma((5,)),
-            dma((10, 8)),
-            dma((10, 8)),
-            dma((8,)),
-            dma((8,)),
-            dma((8,)),
-            dma((8,)),
+            dma((18,)),
+            dma((18,)),
+            dma,
+            dma,
+            dma,
+            dma,
+            dma,
             dma((2,)),
-            dma((2,)),
+            dma,
             dma((3, 2)),
-            dma((3, 2)),
-            dma((8,)),
-            dma((8,)),
-            dma((2,)),
+            dma,
+            dma,
+            dma,
             dma((2,)),
         ],
         compiler_params=pltpu.CompilerParams(

time: 120 us -> 118 us (0.983)
  Pallas kernels: 119 us -> 117 us
    pallas_call x1, Pallas kernels: 117 us -> 116 us  [per_device(): pl.pallas_call(functools.partial(body, Z, N), out_shape=(jax.ShapeDtypeSt...]
where the time goes in v5:
time: 118 us
  Pallas kernels  117 us (99%)
    pallas_call x1, Pallas kernels, per_device(): pl.pallas_call(functools.partial(body, Z, N), out_shape=(jax.ShapeDtypeSt...  116 us

profile of v5, /device:TPU:1, one launch (start us, length us, event | category | flops | bytes accessed | tf_op | source)
XLA Modules:
  0.0 117.9 jit_solution(5434400469008591733)
XLA Ops:
  0.6 115.6 %shard_map.86 = (f32[4,2048]{1,0:T(4,128)}, f32[20,2048]{1,0:T(8,128)}) custom-call(bf16[4,2048]{1,0:T(4,128)(2,1)} %refs_0_.1, bf16[256,512]{1,0:T(8,128)(2,1)} %refs_1_.1, bf16[256,512]{1,0:T(8,128)(2,1)} %refs_2_.1, bf16[20,256]{1,0:T(8,128)(2,1)} %bitcast.1, bf16[2048,512]{1,0:T(8,128)(2,1)} %refs_4_.1, bf16[2048,512]{1,0:T(8,128)(2,1)} %refs_5_.1, ...), custom_call_target="tpu_custom_call" | custom-call | flops 1700000000 | bytes 8000000 | tf_op jit(solution)/shard_map/pallas_call | solution.py:273
  116.2 1.6 %shard_map.87 = (bf16[4,2048]{1,0:T(4,128)(2,1)}, f32[20,2048]{1,0:T(8,128)}) custom-call(f32[4,2048]{1,0:T(4,128)} %get-tuple-element.4.ig, f32[20,2048]{1,0:T(8,128)} %get-tuple-element.5.ad), custom_call_target="tpu_custom_call" | custom-call | tf_op jit(solution)/shard_map/pallas_call | solution.py:324

commit v6 on v5

--- a/solution.py
+++ b/solution.py
@@ -87,27 +87,37 @@
 
     two = 2 - 4 * c
     near = (two, 1, -1)
-    arrivals = (1, -1, 2, -2, 3, -3, 4)
+    arrivals = ((1, -1), (2, -2), (3, -3, 4))
     early = {1: (0, 0, 1), -1: (0, 0, -1), 2: (1, 1, 1), -2: (-1, -1, -1),
              3: (-1, 1, 2), -3: (-1, -1, -2), 4: (2, 2, 2)}
     late = {4: (0, 0, 4), 1: (0, 0, 1), -1: (0, 0, -1), 2: (1, 1, 1), -2: (-1, -1, -1),
             3: (2, 2, 1), -3: (-2, -2, -1)}
 
-    def far_step(buf, sem, tree, m):
+    def far_step(buf, sem, tree, m, whole=False):
         for to, (after, held, step) in tree.items():
             if after == m:
                 blk = buf.at[r, c, (k - held + K) % K]
                 launch(blk, blk, sem.at[0], sem.at[10 + to % K], chip(NEAR * step))
-        blk = buf.at[r, c, (k - m + K) % K]
+        if not whole:
+            near_step(buf.at[r, c, (k - m + K) % K], sem)
+
+    def near_step(blk, sem):
         for n, d in enumerate(near):
             launch(blk, blk, sem.at[1], sem.at[3 + n], chip(d))
 
-    def gather(buf, sem, tree):
-        for m in arrivals:
-            wait_received(buf.at[r, c, (k - m + K) % K], sem.at[10 + m % K])
-            far_step(buf, sem, tree, m)
-        group = buf.at[r, c]
-        launch(group, group, sem.at[2], sem.at[9], sib)
+    def far_gather(*chains):
+        for wave in arrivals:
+            for buf, sem, tree, whole in chains:
+                for m in wave:
+                    wait_received(buf.at[r, c, (k - m + K) % K], sem.at[10 + m % K])
+                    far_step(buf, sem, tree, m, whole)
+                if wave is arrivals[-1]:
+                    group = buf.at[r, c]
+                    if whole:
+                        near_step(group, sem)
+                    launch(group, group, sem.at[2], sem.at[9], sib)
+
+    def near_gather(buf, sem):
         for n, d in ((1, 1), (2, -1), (0, two)):
             got = buf.at[(r - d + NEAR) % NEAR, c]
             wait_received(got, sem.at[3 + n])
@@ -145,7 +155,8 @@
         sigma = jax.nn.sigmoid(gate)
         gate_by[t] = upper * sigma * (1.0 + gate * (1.0 - sigma))
         up_by[t] = gate * sigma
-    gather(abuf, a_sem, early)
+    far_gather((abuf, a_sem, early, False))
+    near_gather(abuf, a_sem)
     from_other_core(abuf, a_sem)
 
     for j in range(K // 2):
@@ -186,77 +197,79 @@
         w = pl.ds(pl.multiple_of(start, 512), 512)
         return (dot_nt(gg, wg_v[w, :]) + dot_nt(ug, wu_v[w, :])).reshape(Z, 8, 512)
 
+    order = sorted(range(K), key=lambda m: -min(m, K - m))
+
+    def rows_of(h, w):
+        own = pown[h, (w + 2 * Z) % Z]
+        return jnp.concatenate([own[:, 0:256], own[:, 256:512]], axis=0)
+
     for h in range(2):
         sibf[h] = part((1 - c) * 1024 + h * 512)
         launch(sibf.at[h], sibr.at[h], ss, sr.at[h], sib)
-    for h in range(2):
         pown[h] = part(c * 1024 + h * 512)
-    for h in range(2):
         wait_received(sibr.at[h], sr.at[h])
         pown[h] = pown[h] + sibr[h]
-
-    order = sorted(range(K), key=lambda m: -min(m, K - m))
-    cut = K // 2
-
-    def rows_of(w):
-        w = (w + 2 * Z) % Z
-        return jnp.concatenate([pown[0, w], pown[1, w]], axis=0)
-
-    for p in range(2):
-        part_m = pl.ds(cut * p, cut)
         for n, d in enumerate(near):
-            for t in range(cut * p, cut * p + cut):
-                csend[n, t] = rows_of(z + d + NEAR * order[t]).astype(BF)
-            launch(csend.at[n, part_m], cnear.at[n, part_m], ns, nr.at[n, p], chip(d))
-    for p in range(2):
-        part_m = pl.ds(cut * p, cut)
-        for n, d in ((1, 1), (2, -1), (0, two)):
-            wait_received(cnear.at[n, part_m], nr.at[n, p])
-        for t in range(cut * p, cut * p + cut):
+            for t in range(K):
+                csend[h, n, t] = rows_of(h, z + d + NEAR * order[t]).astype(BF)
+            launch(csend.at[h, n], cnear.at[h, n], ns, nr.at[h, n], chip(d))
+    others = pl.ds(1, K - 1)
+    last = [None, None]
+    for h in range(2):
+        for n in (1, 2, 0):
+            wait_received(cnear.at[h, n], nr.at[h, n])
+        for t in range(K):
             m = order[t]
-            total = rows_of(z + NEAR * m)
+            total = rows_of(h, z + NEAR * m)
             for n in range(3):
-                total = total + cnear[n, t].astype(F32)
+                total = total + cnear[h, n, t].astype(F32)
             if m:
-                fsend[m] = total.astype(BF)
-                launch(fsend.at[m], cfar.at[m], fs, fr, chip(NEAR * m))
-    others = pl.ds(1, K - 1)
-    wait_received(cfar.at[others], fr)
-    for m in range(1, K):
-        total = total + cfar[m].astype(F32)
-    dbuf[r, c, k] = total.astype(BF)
-
-    far_step(dbuf, d_sem, late, 0)
+                fsend[h, m] = total.astype(BF)
+                launch(fsend.at[h, m], cfar.at[h, m], fs.at[h], fr.at[h], chip(NEAR * m))
+        last[h] = total
+    for h in range(2):
+        total = last[h]
+        wait_received(cfar.at[h, others], fr.at[h])
+        for m in range(1, K):
+            total = total + cfar[h, m].astype(F32)
+        dbuf[h, r, c, k] = total.astype(BF)
+        far_step(dbuf.at[h], d_sem.at[h], late, 0, h == 0)
     gather_sent(abuf, a_sem)
     wait_sent(abuf.at[:, 0], a_sem.at[2])
     wait_sent(hsend.at[pl.ds(0, N - 1)], hs)
     wait_sent(hsum.at[pl.ds(0, N - 1)], gs)
     wait_sent(sibf, ss)
     wait_sent(csend, ns)
-    wait_sent(fsend.at[others], fs)
-    gather(dbuf, d_sem, late)
-
-    def adapter_part(a):
-        x = dbuf[:, a].reshape(2 * rows, 512)
-        eloc[a, 0:20, 0:512] = dot_nn(f0, x)
-        eloc[a, 0:20, 512:1024] = dot_nn(f1, x)
-        launch(eloc.at[a], erem.at[a], es, er.at[a], peer)
-
-    eloc[:, 20:24, :] = jnp.zeros((2, 4, 1024), F32)
-    adapter_part(c)
-    gather_sent(dbuf, d_sem)
-    from_other_core(dbuf, d_sem)
-    adapter_part(1 - c)
-    for a in range(2):
-        blk = dbuf[r, a, k].astype(F32)
-        for h in range(2):
-            block8 = blk[8 * h : 8 * h + 8]
+    for h in range(2):
+        wait_sent(fsend.at[h, others], fs.at[h])
+    eloc[:, :, 20:24, :] = jnp.zeros((2, 2, 4, 512), F32)
+    far_gather(*((dbuf.at[h], d_sem.at[h], late, h == 0) for h in range(2)))
+
+    def adapter_part(h, a):
+        x = dbuf[h, :, a].reshape(2 * rows, 256)
+        eloc[h, a, 0:20, 0:256] = dot_nn(f0, x)
+        eloc[h, a, 0:20, 256:512] = dot_nn(f1, x)
+        launch(eloc.at[h, a], erem.at[h, a], es, er.at[h, a], peer)
+
+    for h in range(2):
+        near_gather(dbuf.at[h], d_sem.at[h])
+        adapter_part(h, c)
+        from_other_core(dbuf.at[h], d_sem.at[h])
+        adapter_part(h, 1 - c)
+    for h in range(2):
+        gather_sent(dbuf.at[h], d_sem.at[h])
+        wait_sent(dbuf.at[h, :, 0], d_sem.at[h, 2])
+        for a in range(2):
+            blk = dbuf[h, r, a, k].astype(F32)
+            for e in range(2):
+                block8 = blk[8 * e : 8 * e + 8]
+                at = 1024 * a + 512 * h + 256 * e
+                ig_out[:, at : at + 256] = jnp.where(c == 0, block8[0:4], block8[4:8])
+    for h in range(2):
+        for a in range(2):
+            wait_received(erem.at[h, a], er.at[h, a])
             at = 1024 * a + 512 * h
-            ig_out[:, at : at + 512] = jnp.where(c == 0, block8[0:4], block8[4:8])
-    wait_sent(dbuf.at[:, 0], d_sem.at[2])
-    for a in range(2):
-        wait_received(erem.at[a], er.at[a])
-        ad_out[:, 1024 * a : 1024 * a + 1024] = eloc[a, 0:20, :] + erem[a, 0:20, :]
+            ad_out[:, at : at + 512] = eloc[h, a, 0:20, :] + erem[h, a, 0:20, :]
     wait_sent(eloc, es)
 
 
@@ -277,7 +290,7 @@
         out_specs=(vmem, vmem),
         scratch_shapes=[
             pltpu.VMEM((NEAR, 2, K, 16, 512), BF),
-            pltpu.VMEM((NEAR, 2, K, 16, 512), BF),
+            pltpu.VMEM((2, NEAR, 2, K, 16, 256), BF),
             pltpu.VMEM((256, 2048), BF),
             pltpu.VMEM((N, 32, 512), F32),
             pltpu.VMEM((N, 32, 512), BF),
@@ -294,15 +307,15 @@
             pltpu.VMEM((2, Z, 8, 512), F32),
             pltpu.VMEM((2, Z, 8, 512), F32),
             pltpu.VMEM((2, Z, 8, 512), F32),
-            pltpu.VMEM((3, K, 16, 512), BF),
-            pltpu.VMEM((3, K, 16, 512), BF),
-            pltpu.VMEM((K, 16, 512), BF),
-            pltpu.VMEM((K, 16, 512), BF),
-            pltpu.VMEM((2, 24, 1024), F32),
-            pltpu.VMEM((2, 24, 1024), F32),
+            pltpu.VMEM((2, 3, K, 16, 256), BF),
+            pltpu.VMEM((2, 3, K, 16, 256), BF),
+            pltpu.VMEM((2, K, 16, 256), BF),
+            pltpu.VMEM((2, K, 16, 256), BF),
+            pltpu.VMEM((2, 2, 24, 512), F32),
+            pltpu.VMEM((2, 2, 24, 512), F32),
             dma((5,)),
             dma((18,)),
-            dma((18,)),
+            dma((2, 18)),
             dma,
             dma,
             dma,
@@ -310,11 +323,11 @@
             dma,
             dma((2,)),
             dma,
-            dma((3, 2)),
-            dma,
-            dma,
-            dma,
+            dma((2, 3)),
             dma((2,)),
+            dma((2,)),
+            dma,
+            dma((2, 2)),
         ],
         compiler_params=pltpu.CompilerParams(
             collective_id=0, has_side_effects=True, vmem_limit_bytes=60 * 1024 * 1024

time: 118 us -> 116 us (0.983)
  Pallas kernels: 117 us -> 115 us
    pallas_call x1, Pallas kernels: 116 us -> 114 us  [per_device(): pl.pallas_call(functools.partial(body, Z, N), out_shape=(jax.ShapeDtypeSt...]
where the time goes in v6:
time: 116 us
  Pallas kernels  115 us (99%)
    pallas_call x1, Pallas kernels, per_device(): pl.pallas_call(functools.partial(body, Z, N), out_shape=(jax.ShapeDtypeSt...  114 us

profile of v6, /device:TPU:1, one launch (start us, length us, event | category | flops | bytes accessed | tf_op | source)
XLA Modules:
  0.0 116.0 jit_solution(86771456297064602)
XLA Ops:
  0.6 113.7 %shard_map.86 = (f32[4,2048]{1,0:T(4,128)}, f32[20,2048]{1,0:T(8,128)}) custom-call(bf16[4,2048]{1,0:T(4,128)(2,1)} %refs_0_.1, bf16[256,512]{1,0:T(8,128)(2,1)} %refs_1_.1, bf16[256,512]{1,0:T(8,128)(2,1)} %refs_2_.1, bf16[20,256]{1,0:T(8,128)(2,1)} %bitcast.1, bf16[2048,512]{1,0:T(8,128)(2,1)} %refs_4_.1, bf16[2048,512]{1,0:T(8,128)(2,1)} %refs_5_.1, ...), custom_call_target="tpu_custom_call" | custom-call | flops 1700000000 | bytes 8000000 | tf_op jit(solution)/shard_map/pallas_call | solution.py:286
  114.4 1.6 %shard_map.87 = (bf16[4,2048]{1,0:T(4,128)(2,1)}, f32[20,2048]{1,0:T(8,128)}) custom-call(f32[4,2048]{1,0:T(4,128)} %get-tuple-element.4.ig, f32[20,2048]{1,0:T(8,128)} %get-tuple-element.5.ad), custom_call_target="tpu_custom_call" | custom-call | tf_op jit(solution)/shard_map/pallas_call | solution.py:337

commit v7 on v6

--- a/solution.py
+++ b/solution.py
@@ -165,30 +165,33 @@
         for q in range(4):
             full[64 * j : 64 * j + 64, 512 * q : 512 * q + 512] = out[64 * q : 64 * q + 64]
     local[0].wait()
-    hpart[...] = dot_nt(full[...], wd_v[...]).reshape(hpart.shape)
-    hsend[...] = hpart[...].astype(BF)
-
-    for j in range(1, N):
-        launch(hsend.at[(inp + j) % N], hrecv.at[j - 1], hs, hr, ring(j))
-    total = hpart[inp]
-    wait_received(hrecv, hr)
-    for j in range(1, N):
-        total = total + hrecv[j - 1].astype(F32)
-    hsum[inp] = total.astype(BF)
-    for j in range(1, N):
-        launch(hsum.at[inp], hsum.at[inp], gs, gr, ring(j))
-
-    def grads(t):
-        h = hsum[t].astype(F32)
-        gu[0, t] = (h * gate_by[t]).astype(BF)
-        gu[1, t] = (h * up_by[t]).astype(BF)
-
-    grads(inp)
+    for g in range(2):
+        hpart[g] = dot_nt(full[...], wd_v[256 * g : 256 * g + 256, :]).reshape(N, 32, 256)
+        hsend[g] = hpart[g].astype(BF)
+        for j in range(1, N):
+            launch(hsend.at[g, (inp + j) % N], hrecv.at[g, j - 1], hs.at[g], hr.at[g], ring(j))
+    for g in range(2):
+        total = hpart[g, inp]
+        wait_received(hrecv.at[g], hr.at[g])
+        for j in range(1, N):
+            total = total + hrecv[g, j - 1].astype(F32)
+        hsum[g, inp] = total.astype(BF)
+        for j in range(1, N):
+            launch(hsum.at[g, inp], hsum.at[g, inp], gs.at[g], gr.at[g], ring(j))
+
+    def grads(g, t):
+        h = hsum[g, t].astype(F32)
+        cols = pl.ds(256 * g, 256)
+        gu[0, t, :, cols] = (h * gate_by[t, :, cols]).astype(BF)
+        gu[1, t, :, cols] = (h * up_by[t, :, cols]).astype(BF)
+
     local[3].wait()
     local[4].wait()
-    wait_received(hsum.at[pl.ds(0, N - 1)], gr)
-    for j in range(1, N):
-        grads((inp - j + N) % N)
+    for g in range(2):
+        grads(g, inp)
+        wait_received(hsum.at[g, pl.ds(0, N - 1)], gr.at[g])
+        for j in range(1, N):
+            grads(g, (inp - j + N) % N)
 
     gg = gu[0].reshape(256, 512)
     ug = gu[1].reshape(256, 512)
@@ -236,8 +239,9 @@
         far_step(dbuf.at[h], d_sem.at[h], late, 0, h == 0)
     gather_sent(abuf, a_sem)
     wait_sent(abuf.at[:, 0], a_sem.at[2])
-    wait_sent(hsend.at[pl.ds(0, N - 1)], hs)
-    wait_sent(hsum.at[pl.ds(0, N - 1)], gs)
+    for g in range(2):
+        wait_sent(hsend.at[g, pl.ds(0, N - 1)], hs.at[g])
+        wait_sent(hsum.at[g, pl.ds(0, N - 1)], gs.at[g])
     wait_sent(sibf, ss)
     wait_sent(csend, ns)
     for h in range(2):
@@ -292,10 +296,10 @@
             pltpu.VMEM((NEAR, 2, K, 16, 512), BF),
             pltpu.VMEM((2, NEAR, 2, K, 16, 256), BF),
             pltpu.VMEM((256, 2048), BF),
-            pltpu.VMEM((N, 32, 512), F32),
-            pltpu.VMEM((N, 32, 512), BF),
-            pltpu.VMEM((N - 1, 32, 512), BF),
-            pltpu.VMEM((N, 32, 512), BF),
+            pltpu.VMEM((2, N, 32, 256), F32),
+            pltpu.VMEM((2, N, 32, 256), BF),
+            pltpu.VMEM((2, N - 1, 32, 256), BF),
+            pltpu.VMEM((2, N, 32, 256), BF),
             pltpu.VMEM((N, 32, 512), F32),
             pltpu.VMEM((N, 32, 512), F32),
             pltpu.VMEM((2, N, 32, 512), BF),
@@ -316,10 +320,10 @@
             dma((5,)),
             dma((18,)),
             dma((2, 18)),
-            dma,
-            dma,
-            dma,
-            dma,
+            dma((2,)),
+            dma((2,)),
+            dma((2,)),
+            dma((2,)),
             dma,
             dma((2,)),
             dma,

time: 116 us -> 116 us (level)
  no operation moved by 1% of the time
where the time goes in v7:
time: 116 us
  Pallas kernels  115 us (99%)
    pallas_call x1, Pallas kernels, per_device(): pl.pallas_call(functools.partial(body, Z, N), out_shape=(jax.ShapeDtypeSt...  113 us

profile of v7, /device:TPU:1, one launch (start us, length us, event | category | flops | bytes accessed | tf_op | source)
XLA Modules:
  0.0 115.6 jit_solution(3346647945655873509)
XLA Ops:
  0.6 113.3 %shard_map.86 = (f32[4,2048]{1,0:T(4,128)}, f32[20,2048]{1,0:T(8,128)}) custom-call(bf16[4,2048]{1,0:T(4,128)(2,1)} %refs_0_.1, bf16[256,512]{1,0:T(8,128)(2,1)} %refs_1_.1, bf16[256,512]{1,0:T(8,128)(2,1)} %refs_2_.1, bf16[20,256]{1,0:T(8,128)(2,1)} %bitcast.1, bf16[2048,512]{1,0:T(8,128)(2,1)} %refs_4_.1, bf16[2048,512]{1,0:T(8,128)(2,1)} %refs_5_.1, ...), custom_call_target="tpu_custom_call" | custom-call | flops 1700000000 | bytes 8000000 | tf_op jit(solution)/shard_map/pallas_call | solution.py:290
  113.9 1.6 %shard_map.87 = (bf16[4,2048]{1,0:T(4,128)(2,1)}, f32[20,2048]{1,0:T(8,128)}) custom-call(f32[4,2048]{1,0:T(4,128)} %get-tuple-element.4.ig, f32[20,2048]{1,0:T(8,128)} %get-tuple-element.5.ad), custom_call_target="tpu_custom_call" | custom-call | tf_op jit(solution)/shard_map/pallas_call | solution.py:341

commit v8 on v7

--- a/solution.py
+++ b/solution.py
@@ -185,6 +185,13 @@
         gu[0, t, :, cols] = (h * gate_by[t, :, cols]).astype(BF)
         gu[1, t, :, cols] = (h * up_by[t, :, cols]).astype(BF)
 
+    def part(start, g):
+        w = pl.ds(pl.multiple_of(start, 512), 512)
+        cols = pl.ds(256 * g, 256)
+        gg = gu[0, :, :, cols].reshape(256, 256)
+        ug = gu[1, :, :, cols].reshape(256, 256)
+        return (dot_nt(gg, wg_v[w, cols]) + dot_nt(ug, wu_v[w, cols])).reshape(Z, 8, 512)
+
     local[3].wait()
     local[4].wait()
     for g in range(2):
@@ -192,13 +199,9 @@
         wait_received(hsum.at[g, pl.ds(0, N - 1)], gr.at[g])
         for j in range(1, N):
             grads(g, (inp - j + N) % N)
-
-    gg = gu[0].reshape(256, 512)
-    ug = gu[1].reshape(256, 512)
-
-    def part(start):
-        w = pl.ds(pl.multiple_of(start, 512), 512)
-        return (dot_nt(gg, wg_v[w, :]) + dot_nt(ug, wu_v[w, :])).reshape(Z, 8, 512)
+        if g == 0:
+            sibf[0] = part((1 - c) * 1024, 0)
+            pown[0] = part(c * 1024, 0)
 
     order = sorted(range(K), key=lambda m: -min(m, K - m))
 
@@ -207,9 +210,10 @@
         return jnp.concatenate([own[:, 0:256], own[:, 256:512]], axis=0)
 
     for h in range(2):
-        sibf[h] = part((1 - c) * 1024 + h * 512)
+        away, here = (1 - c) * 1024 + h * 512, c * 1024 + h * 512
+        sibf[h] = part(away, 1) + (sibf[h] if h == 0 else part(away, 0))
         launch(sibf.at[h], sibr.at[h], ss, sr.at[h], sib)
-        pown[h] = part(c * 1024 + h * 512)
+        pown[h] = part(here, 1) + (pown[h] if h == 0 else part(here, 0))
         wait_received(sibr.at[h], sr.at[h])
         pown[h] = pown[h] + sibr[h]
         for n, d in enumerate(near):

time: 116 us -> 116 us (level)
  no operation moved by 1% of the time
where the time goes in v8:
time: 116 us; the launch traced here: 115 us
  Pallas kernels  115 us (99%)
    pallas_call x1, Pallas kernels, per_device(): pl.pallas_call(functools.partial(body, Z, N), out_shape=(jax.ShapeDtypeSt...  113 us

profile of v8, /device:TPU:1, one launch (start us, length us, event | category | flops | bytes accessed | tf_op | source)
XLA Modules:
  0.0 115.4 jit_solution(8126805726503993610)
XLA Ops:
  0.6 113.1 %shard_map.86 = (f32[4,2048]{1,0:T(4,128)}, f32[20,2048]{1,0:T(8,128)}) custom-call(bf16[4,2048]{1,0:T(4,128)(2,1)} %refs_0_.1, bf16[256,512]{1,0:T(8,128)(2,1)} %refs_1_.1, bf16[256,512]{1,0:T(8,128)(2,1)} %refs_2_.1, bf16[20,256]{1,0:T(8,128)(2,1)} %bitcast.1, bf16[2048,512]{1,0:T(8,128)(2,1)} %refs_4_.1, bf16[2048,512]{1,0:T(8,128)(2,1)} %refs_5_.1, ...), custom_call_target="tpu_custom_call" | custom-call | flops 1700000000 | bytes 8000000 | tf_op jit(solution)/shard_map/pallas_call | solution.py:294
  113.7 1.6 %shard_map.87 = (bf16[4,2048]{1,0:T(4,128)(2,1)}, f32[20,2048]{1,0:T(8,128)}) custom-call(f32[4,2048]{1,0:T(4,128)} %get-tuple-element.4.ig, f32[20,2048]{1,0:T(8,128)} %get-tuple-element.5.ad), custom_call_target="tpu_custom_call" | custom-call | tf_op jit(solution)/shard_map/pallas_call | solution.py:345
